TPU v7x, 32 devices: a whole 2x2x4 slice. The times are simulated.
32 devices in a mesh: band: 8 (over z, y), lon: 4 (over x, core).
Axes of the slice: x: 2, y: 2, z: 4, core: 2. Of those that a mesh axis runs over, the one named last changes fastest.
Arguments:
- node_state: bfloat16 [65536, 64], P(('band', 'lon')), may hold values from -6 to 6
- latent: bfloat16 [65536, 64], P(('band', 'lon')), may hold values from -6 to 6
- edge_attr: bfloat16 [2, 65536, 8, 64], P(None, ('band', 'lon')), may hold values from -6 to 6
- neighbours: int32 [2, 65536, 8], P(None, ('band', 'lon')), may hold values from 0 to 2559
- halo_lists: int32 [128, 128], P(('band', 'lon')), may hold values from 0 to 1023
- valid_counts: int32 [32], P(('band', 'lon')), may hold values from 1024 to 2048
- channel_mask: int32 [2, 64], replicated, may hold values 0 or 1
- edge_w1: bfloat16 [2, 192, 64], replicated, may hold values from -0.4375 to 0.4375
- edge_b1: float32 [2, 64], replicated, may hold values from -3 to 3
- edge_w2: bfloat16 [2, 64, 64], replicated, may hold values from -0.75 to 0.75
- edge_gain: float32 [2, 64], replicated, may hold values from 0.25 to 1.75
- edge_shift: float32 [2, 64], replicated, may hold values from -2 to 2
- node_w1: bfloat16 [2, 128, 64], replicated, may hold values from -0.5 to 0.5
- node_b1: float32 [2, 64], replicated, may hold values from -3 to 3
- node_w2: bfloat16 [2, 64, 64], replicated, may hold values from -0.75 to 0.75
- node_gain: float32 [2, 64], replicated, may hold values from 0.25 to 1.75
- node_shift: float32 [2, 64], replicated, may hold values from -2 to 2
- out_grad: bfloat16 [65536, 64], P(('band', 'lon')), may hold values from -6 to 6
Outputs:
- mesh_out: bfloat16 [65536, 64], P(('band', 'lon'))
- grad_state: float32 [65536, 64], P(('band', 'lon'))
- grad_latent: float32 [65536, 64], P(('band', 'lon'))
- grad_edge_w1: float32 [2, 192, 64], replicated
- grad_edge_b1: float32 [2, 64], replicated
- grad_edge_w2: float32 [2, 64, 64], replicated
- grad_edge_gain: float32 [2, 64], replicated
- grad_edge_shift: float32 [2, 64], replicated
- grad_node_w1: float32 [2, 128, 64], replicated
- grad_node_b1: float32 [2, 64], replicated
- grad_node_w2: float32 [2, 64, 64], replicated
- grad_node_gain: float32 [2, 64], replicated
- grad_node_shift: float32 [2, 64], replicated
Inputs may be any that keep to these rules, and one draw needn't show every extreme that they name: `neighbours`: values below 2048 name this device's own rows; the next four blocks of 128 name the rows from the band below, the band above, the sector west and the sector east, in order. `halo_lists`: rows of the device itself, always below its live count.
All inputs are finite; a program needn't handle non-finite values.
Results may differ from a plain program's by a relative error of at most 0.012.
Values may be sent and summed in bfloat16 or wider, within the bound.
A program may use at most 128 MiB of HBM per device.

v0:
```python
import math

import jax
import jax.numpy as jnp
from jax import lax
from jax.sharding import PartitionSpec as P


def extended(block, sides, width, periodic):
    for axis, dim in sides:
        count = lax.axis_size(axis)
        forward = [(i, i + 1) for i in range(count - 1)]
        if periodic:
            forward.append((count - 1, 0))
        backward = [(target, source) for source, target in forward]
        low = lax.ppermute(
            lax.slice_in_dim(block, block.shape[dim] - width, None, axis=dim), axis, forward
        )
        high = lax.ppermute(lax.slice_in_dim(block, 0, width, axis=dim), axis, backward)
        block = jnp.concatenate([low, block, high], axis=dim)
    return block


def matmul(left, right):
    return jnp.dot(left, right, preferred_element_type=jnp.float32)


def exact_matmul(left, right):
    return jnp.dot(left, right, precision=lax.Precision.HIGHEST, preferred_element_type=jnp.float32)


def normalize(values):
    center = values - jnp.mean(values, axis=-1, keepdims=True)
    rate = lax.rsqrt(jnp.mean(center * center, axis=-1, keepdims=True) + 1e-05)
    return (center * rate, rate)


def norm_back(grad_unit, unit, rate):
    return rate * (
        grad_unit
        - jnp.mean(grad_unit, axis=-1, keepdims=True)
        - unit * jnp.mean(grad_unit * unit, axis=-1, keepdims=True)
    )


def silu_slope(values):
    sigma = jax.nn.sigmoid(values)
    return sigma * (1.0 + values * (1.0 - sigma))


def one_hot_rows(index, total, kind):
    return (index[:, None] == jnp.arange(total, dtype=jnp.int32)[None, :]).astype(kind)


def gather_rows(source, index):
    edges = index.shape[0]
    block = math.gcd(edges, 512)
    blocks = index.reshape(edges // block, block)
    total = source.shape[0]

    def pick_block(block_index):
        return matmul(one_hot_rows(block_index, total, jnp.bfloat16), source).astype(jnp.bfloat16)

    picked = lax.map(pick_block, blocks)
    return picked.reshape(edges, source.shape[1])


def scatter_rows(values, index, total):
    edges = index.shape[0]
    block = math.gcd(edges, 512)
    blocks = index.reshape(edges // block, block)
    value_blocks = values.reshape(edges // block, block, values.shape[1])

    def add_block(carry, pieces):
        block_index, block_values = pieces
        selector = one_hot_rows(block_index, total, jnp.bfloat16)
        term = lax.dot_general(
            selector, block_values, (((0,), (0,)), ((), ())), preferred_element_type=jnp.float32
        )
        return (carry + term, None)

    start = jnp.zeros((total, values.shape[1]), jnp.float32)
    summed, unused = lax.scan(add_block, start, (blocks, value_blocks))
    return summed


def build_table(node_low, lists):
    halo_rows = lists.shape[1]
    picked = gather_rows(node_low, lists.reshape(-1)).reshape(4, halo_rows, node_low.shape[1])
    band_pad = extended(picked[0:2], (("band", 0),), 1, False)
    sector_pad = extended(picked[2:4], (("lon", 0),), 1, True)
    return jnp.concatenate(
        [node_low, band_pad[0], band_pad[3], sector_pad[0], sector_pad[3]], axis=0
    )


def edge_forward(table, node_low, neighbour, attribute, params):
    width = node_low.shape[1]
    node_rows, degree = neighbour.shape
    first = params[0]
    senders = gather_rows(table, neighbour.reshape(-1))
    sender_part = matmul(senders, first[:width]).reshape(node_rows, degree, width)
    receiver_part = matmul(node_low, first[width : 2 * width])
    attr_part = matmul(attribute.reshape(node_rows * degree, width), first[2 * width :]).reshape(
        node_rows, degree, width
    )
    pre_one = sender_part + receiver_part[:, None, :] + attr_part + params[1]
    act_one = jax.nn.silu(pre_one).astype(jnp.bfloat16)
    pre_two = matmul(act_one.reshape(node_rows * degree, width), params[2]).reshape(
        node_rows, degree, width
    )
    return (pre_one, act_one, pre_two)


def forward_layer(state, params, neighbour, attribute, scale, valid, lists):
    width = state.shape[1]
    node_low = state.astype(jnp.bfloat16)
    table = build_table(node_low, lists)
    pre_one, act_one, pre_two = edge_forward(table, node_low, neighbour, attribute, params)
    unit_two, rate_two = normalize(pre_two)
    message = (unit_two * params[3] + params[4]) * scale
    summed_low = jnp.sum(message, axis=1).astype(jnp.bfloat16)
    pre_three = (
        matmul(node_low, params[5][:width]) + matmul(summed_low, params[5][width:]) + params[6]
    )
    act_three = jax.nn.silu(pre_three).astype(jnp.bfloat16)
    pre_four = matmul(act_three, params[7])
    unit_four, rate_four = normalize(pre_four)
    result = state + valid[:, None] * (unit_four * params[8] + params[9])
    kept = (pre_one, act_one, pre_two)
    return (result, (node_low, table, summed_low, pre_three, act_three, unit_four, rate_four, kept))


def backward_layer(grad_out, cache, params, neighbour, attribute, scale, valid, lists):
    node_low, table, summed_low, pre_three, act_three, unit_four, rate_four, kept = cache
    node_rows, degree = neighbour.shape
    width = node_low.shape[1]
    pre_one, act_one, pre_two = kept
    unit_two, rate_two = normalize(pre_two)
    grad_norm = valid[:, None] * grad_out
    grad_node_gain = jnp.sum(grad_norm * unit_four, axis=0)
    grad_node_shift = jnp.sum(grad_norm, axis=0)
    grad_four = norm_back(grad_norm * params[8], unit_four, rate_four).astype(jnp.bfloat16)
    grad_node_w2 = matmul(act_three.T, grad_four)
    grad_act_three = matmul(grad_four, params[7].T)
    grad_three = (grad_act_three * silu_slope(pre_three)).astype(jnp.bfloat16)
    grad_node_b1 = jnp.sum(grad_three.astype(jnp.float32), axis=0)
    grad_node_w1 = jnp.concatenate(
        [matmul(node_low.T, grad_three), matmul(summed_low.T, grad_three)], axis=0
    )
    grad_state = grad_out + matmul(grad_three, params[5][:width].T)
    grad_summed = matmul(grad_three, params[5][width:].T)
    grad_message = grad_summed[:, None, :] * scale
    grad_edge_gain = jnp.sum(grad_message * unit_two, axis=(0, 1))
    grad_edge_shift = jnp.sum(grad_message, axis=(0, 1))
    grad_two = norm_back(grad_message * params[3], unit_two, rate_two).astype(jnp.bfloat16)
    grad_two_flat = grad_two.reshape(node_rows * degree, width)
    grad_edge_w2 = matmul(act_one.reshape(node_rows * degree, width).T, grad_two_flat)
    grad_act_one = matmul(grad_two_flat, params[2].T).reshape(node_rows, degree, width)
    grad_one = (grad_act_one * silu_slope(pre_one)).astype(jnp.bfloat16)
    grad_edge_b1 = jnp.sum(grad_one.astype(jnp.float32), axis=(0, 1))
    grad_one_flat = grad_one.reshape(node_rows * degree, width)
    table_rows = table.shape[0]
    gathered_grad = scatter_rows(grad_one_flat, neighbour.reshape(-1), table_rows)
    grad_sender_w = exact_matmul(table.astype(jnp.float32).T, gathered_grad)
    grad_receiver_w = (
        matmul(node_low.T, grad_one.reshape(node_rows, degree * width))
        .reshape(width, degree, width)
        .sum(axis=1)
    )
    grad_attr_w = matmul(attribute.reshape(node_rows * degree, width).T, grad_one_flat)
    grad_edge_w1 = jnp.concatenate([grad_sender_w, grad_receiver_w, grad_attr_w], axis=0)
    grad_state = grad_state + matmul(grad_one_flat, params[0][width : 2 * width].T).reshape(
        node_rows, degree, width
    ).sum(axis=1)
    grad_table = exact_matmul(gathered_grad, params[0][:width].astype(jnp.float32).T)
    grad_state = grad_state + grad_table[:node_rows]
    halo_rows = lists.shape[1]
    grad_halo = grad_table[node_rows:].reshape(4, halo_rows, width)
    band_back = extended(grad_halo[0:2].astype(jnp.bfloat16), (("band", 0),), 1, False).astype(
        jnp.float32
    )
    sector_back = extended(grad_halo[2:4].astype(jnp.bfloat16), (("lon", 0),), 1, True).astype(
        jnp.float32
    )
    returned = jnp.concatenate([band_back[0], band_back[3], sector_back[0], sector_back[3]], axis=0)
    owner = one_hot_rows(lists.reshape(-1), node_rows, jnp.float32)
    grad_state = grad_state + exact_matmul(owner.T, returned)
    grads = (
        grad_edge_w1,
        grad_edge_b1,
        grad_edge_w2,
        grad_edge_gain,
        grad_edge_shift,
        grad_node_w1,
        grad_node_b1,
        grad_node_w2,
        grad_node_gain,
        grad_node_shift,
    )
    return (grad_state, grads)


def reduce_layer(grads):
    return lax.psum(grads, ("band", "lon"))


def shards(
    node_state,
    latent,
    edge_attr,
    neighbours,
    halo_lists,
    valid_counts,
    channel_mask,
    edge_w1,
    edge_b1,
    edge_w2,
    edge_gain,
    edge_shift,
    node_w1,
    node_b1,
    node_w2,
    node_gain,
    node_shift,
    out_grad,
):
    node_rows = node_state.shape[0]
    halo_rows = halo_lists.shape[1]
    count = valid_counts[0]
    receiver_ok = jnp.arange(node_rows, dtype=jnp.int32) < count
    valid = receiver_ok.astype(jnp.float32)
    band_at = lax.axis_index("band")
    band_total = lax.axis_size("band")
    weights = (
        edge_w1,
        edge_b1,
        edge_w2,
        edge_gain,
        edge_shift,
        node_w1,
        node_b1,
        node_w2,
        node_gain,
        node_shift,
    )

    def layer_inputs(layer_at):
        neighbour = neighbours[layer_at]
        sender_ok = jnp.where(
            neighbour < node_rows,
            neighbour < count,
            jnp.where(
                neighbour < node_rows + halo_rows,
                band_at > 0,
                jnp.where(neighbour < node_rows + 2 * halo_rows, band_at < band_total - 1, True),
            ),
        )
        edge_ok = (sender_ok & receiver_ok[:, None]).astype(jnp.float32)
        scale = edge_ok[..., None] * channel_mask[layer_at].astype(jnp.float32)
        params = tuple((item[layer_at] for item in weights))
        return (params, neighbour, edge_attr[layer_at], scale)

    params_low, neighbour_low, attr_low, scale_low = layer_inputs(0)
    params_high, neighbour_high, attr_high, scale_high = layer_inputs(1)
    middle, cache_low = forward_layer(
        node_state.astype(jnp.float32),
        params_low,
        neighbour_low,
        attr_low,
        scale_low,
        valid,
        halo_lists,
    )
    middle = middle + latent.astype(jnp.float32)
    top, cache_high = forward_layer(
        middle, params_high, neighbour_high, attr_high, scale_high, valid, halo_lists
    )
    grad_latent, grads_high = backward_layer(
        out_grad.astype(jnp.float32),
        cache_high,
        params_high,
        neighbour_high,
        attr_high,
        scale_high,
        valid,
        halo_lists,
    )
    grads_high = reduce_layer(grads_high)
    grad_state, grads_low = backward_layer(
        grad_latent, cache_low, params_low, neighbour_low, attr_low, scale_low, valid, halo_lists
    )
    grads_low = reduce_layer(grads_low)
    stacked = tuple((jnp.stack([first, second]) for first, second in zip(grads_low, grads_high)))
    return (
        top.astype(jnp.bfloat16),
        grad_state,
        grad_latent,
        stacked[0],
        stacked[1],
        stacked[2],
        stacked[3],
        stacked[4],
        stacked[5],
        stacked[6],
        stacked[7],
        stacked[8],
        stacked[9],
    )


def solution(mesh):
    in_specs = (
        P(("band", "lon"), None),
        P(("band", "lon"), None),
        P(None, ("band", "lon"), None, None),
        P(None, ("band", "lon"), None),
        P(("band", "lon"), None),
        P(("band", "lon")),
        P(),
        P(),
        P(),
        P(),
        P(),
        P(),
        P(),
        P(),
        P(),
        P(),
        P(),
        P(("band", "lon"), None),
    )
    out_specs = (
        P(("band", "lon"), None),
        P(("band", "lon"), None),
        P(("band", "lon"), None),
        P(),
        P(),
        P(),
        P(),
        P(),
        P(),
        P(),
        P(),
        P(),
        P(),
    )
    return jax.shard_map(shards, mesh=mesh, in_specs=in_specs, out_specs=out_specs, check_vma=False)
```

profile of v0, /device:TPU:0, one launch (start us, length us, event | category | flops | bytes accessed | tf_op | source)
XLA Modules:
  0.0 779.1 jit_solution(13513826666264675014)
XLA Ops:
  9.8 5.5 collective-permute-start
  21.7 4.3 fusion.78
  26.0 3.3 fusion.76
  43.4 2.4 reshape_reshape_squeeze.9
  45.8 6.1 copy.114
  51.9 4.3 copy.117
  59.8 40.4 %while.50 = (s32[]{:T(128)}, bf16[32,512,64]{1,2,0:T(8,128)(2,1)S(1)}, s32[32,512]{1,0:T(8,128)S(1)}, bf16[2560,64]{1,0:T(8,128)(2,1)S(1)}, s32[]{:T(128)}) while((s32[]{:T(128)}, bf16[32,512,64]{1,2,0:T(8,128)(2,1)S(1)}, s32[32,512]{1,0:T(8,128)S(1)}, bf16[2560,64]{1,0:T(8,128)(2,1)S(1)}, s32[]{:T(128)}) %tuple.138), condition=%wide.region_1.2_spmd, body=%wide.region_0.1_spmd.sunk | while | flops 169115648 | bytes 727109 | solution.py:64
  100.3 3.2 copy.91
  103.5 7.7 multiply_convert_fusion.3
  117.8 4.6 collective-permute-start.4
  126.5 2.5 collective-permute-done.5
  131.2 97.8 %while.51 = (s32[]{:T(128)}, bf16[32,512,64]{1,2,0:T(8,128)(2,1)S(1)}, s32[32,512]{1,0:T(8,128)}, bf16[2560,64]{1,0:T(8,128)(2,1)}, s32[]{:T(128)}) while((s32[]{:T(128)}, bf16[32,512,64]{1,2,0:T(8,128)(2,1)S(1)}, s32[32,512]{1,0:T(8,128)}, bf16[2560,64]{1,0:T(8,128)(2,1)}, s32[]{:T(128)}) %tuple.141), condition=%wide.region_8.9_spmd, body=%wide.region_7.8_spmd.sunk | while | flops 169115648 | bytes 399429 | solution.py:64
  141.2 2.3 fusion.278
  229.0 3.2 copy.97
  232.2 5.7 multiply_convert_fusion.2
  243.9 2.5 fusion.44
  247.9 2.8 convert_reduce_fusion
  250.7 4.4 copy.102
  255.2 145.4 %while.52 = (s32[]{:T(128)}, f32[2560,64]{0,1:T(8,128)}, s32[32,512]{1,0:T(8,128)}, bf16[32,512,64]{2,1,0:T(8,128)(2,1)}, s32[]{:T(128)}, /*index=5*/s32[]{:T(128)}) while((s32[]{:T(128)}, f32[2560,64]{0,1:T(8,128)}, s32[32,512]{1,0:T(8,128)}, bf16[32,512,64]{2,1,0:T(8,128)(2,1)}, s32[]{:T(128)}, /*index=5*/s32[]{:T(128)}) %tuple.157), condition=%wide.region_20.21_spmd.clone, body=%wide.region_19.20_spmd.clone.sunk | while | flops 169410560 | bytes 1448531 | solution.py:83
  256.5 3.0 fusion.280
  260.8 3.3 fusion.280
  265.3 3.3 fusion.280
  269.9 3.3 fusion.280
  274.4 3.3 fusion.280
  279.0 3.3 fusion.280
  283.5 3.3 fusion.280
  288.1 3.3 fusion.280
  292.6 3.3 fusion.280
  297.2 3.3 fusion.280
  301.7 3.3 fusion.280
  306.3 3.3 fusion.280
  310.8 3.3 fusion.280
  315.4 3.3 fusion.280
  319.9 3.3 fusion.280
  324.5 3.3 fusion.280
  329.0 3.3 fusion.280
  333.6 3.3 fusion.280
  338.1 3.3 fusion.280
  342.7 3.3 fusion.280
  347.2 3.3 fusion.280
  351.8 3.3 fusion.280
  356.3 3.3 fusion.280
  360.9 3.3 fusion.280
  365.4 3.3 fusion.280
  370.0 3.3 fusion.280
  374.5 3.3 fusion.280
  379.1 3.3 fusion.280
  383.6 3.3 fusion.280
  388.2 3.3 fusion.280
  392.8 3.3 fusion.280
  397.3 3.3 fusion.280
  400.6 2.6 fusion.212
  404.4 2.4 convolution_reduce_fusion.1
  414.4 4.6 collective-permute-start.8
  423.2 4.8 fusion.94
  430.2 2.4 multiply_reduce_fusion.2
  438.8 2.8 fusion.38
  444.5 2.7 convert_reduce_fusion.1
  447.2 4.3 copy.108
  451.5 92.9 %while.53 = (s32[]{:T(128)}, f32[2560,64]{0,1:T(8,128)S(1)}, s32[32,512]{1,0:T(8,128)}, bf16[32,512,64]{2,1,0:T(8,128)(2,1)}, s32[]{:T(128)}, /*index=5*/s32[]{:T(128)}) while((s32[]{:T(128)}, f32[2560,64]{0,1:T(8,128)S(1)}, s32[32,512]{1,0:T(8,128)}, bf16[32,512,64]{2,1,0:T(8,128)(2,1)}, s32[]{:T(128)}, ...), condition=%wide.region_27.28_spmd.clone, body=%wide.region_26.27_spmd.clone.sunk | while | flops 169410560 | bytes 1448531 | solution.py:83
  550.9 4.2 fusion.89
  557.6 4.5 collective-permute-start.12
  571.6 3.2 fusion.65
  574.8 183.8 %all-reduce.3.cloned.1.call-done = (f32[1,192,64]{1,2,0:T(8,128)}, f32[1,192,64]{1,2,0:T(8,128)}, f32[1,64]{1,0:T(1,128)}, f32[1,64]{1,0:T(1,128)}, f32[1,64,64]...) async-done(((f32[1,192,64]{1,2,0:T(8,128)}, ...) | async-done | bytes 232464 | tf_op jit(solution)/shard_map/psum | solution.py:205
  (561 shorter events, 368.8 us)
Async XLA Ops:
  7.2 751.5 %all-reduce.3.cloned.1.call-start = ((), (), s32[]{:S(2)}) async-start(), calls=%async_computation | async-start | bytes 667648 | tf_op jit(solution)/shard_map/psum | solution.py:205
  9.8 46.4 %collective-permute-start = (bf16[1,128,64]{1,2,0:T(8,128)(2,1)}, bf16[1,128,64]{1,2,0:T(8,128)(2,1)}, u32[]{:S(2)}, u32[]{:S(2)}) collective-permute-start(bf16[1,128,64]{1,2,0:T(8,128)(2,1)} %get-tuple-element.276), channel_id=1, source_target_pairs={{0,4},{4,8},{8,12},{12,16},{16,20},{20,24},{24,28},{1,5},{5,9},{9,... | collective-permute-start | bytes 49160 | tf_op jit(solution)/shard_map/ppermute | solution.py:16
  15.2 41.8 %collective-permute-start.1 = (bf16[1,128,64]{1,2,0:T(8,128)(2,1)}, bf16[1,128,64]{1,2,0:T(8,128)(2,1)}, u32[]{:S(2)}, u32[]{:S(2)}) collective-permute-start(bf16[1,128,64]{1,2,0:T(8,128)(2,1)} %get-tuple-element.275), channel_id=1, source_target_pairs={{4,0},{8,4},{12,8},{16,12},{20,16},{24,20},{28,24},{5,1},{9,5},{13... | collective-permute-start | bytes 49160 | tf_op jit(solution)/shard_map/ppermute | solution.py:19
  16.5 41.3 %collective-permute-start.2 = (bf16[1,128,64]{1,2,0:T(8,128)(2,1)}, bf16[1,128,64]{1,2,0:T(8,128)(2,1)}, u32[]{:S(2)}, u32[]{:S(2)}) collective-permute-start(bf16[1,128,64]{1,2,0:T(8,128)(2,1)} %get-tuple-element.274), channel_id=1, source_target_pairs={{0,1},{1,2},{2,3},{3,0},{4,5},{5,6},{6,7},{7,4},{8,9},{9,10},{10,1... | collective-permute-start | bytes 49160 | tf_op jit(solution)/shard_map/ppermute | solution.py:16
  16.6 42.1 %collective-permute-start.3 = (bf16[1,128,64]{1,2,0:T(8,128)(2,1)}, bf16[1,128,64]{1,2,0:T(8,128)(2,1)}, u32[]{:S(2)}, u32[]{:S(2)}) collective-permute-start(bf16[1,128,64]{1,2,0:T(8,128)(2,1)} %get-tuple-element.273), channel_id=1, source_target_pairs={{1,0},{2,1},{3,2},{0,3},{5,4},{6,5},{7,6},{4,7},{9,8},{10,9},{11,1... | collective-permute-start | bytes 49160 | tf_op jit(solution)/shard_map/ppermute | solution.py:19
  19.5 6.5 copy-start.3
  32.4 80.3 %copy-start.69 = (f32[64]{0:T(128)}, f32[64]{0:T(128)S(1)}, u32[]{:S(2)}) copy-start(f32[64]{0:T(128)S(1)} %get-tuple-element.286) | copy-start | bytes 772
  32.4 207.0 %copy-start.71 = (f32[64]{0:T(128)}, f32[64]{0:T(128)S(1)}, u32[]{:S(2)}) copy-start(f32[64]{0:T(128)S(1)} %get-tuple-element.285) | copy-start | bytes 772
  35.4 77.3 %copy-start.73 = (f32[64]{0:T(128)}, f32[64]{0:T(128)S(1)}, u32[]{:S(2)}) copy-start(f32[64]{0:T(128)S(1)} %get-tuple-element.322) | copy-start | bytes 772
  35.4 204.0 %copy-start.75 = (f32[64]{0:T(128)}, f32[64]{0:T(128)S(1)}, u32[]{:S(2)}) copy-start(f32[64]{0:T(128)S(1)} %get-tuple-element.323) | copy-start | bytes 772
  37.7 75.0 %copy-start.27 = (f32[2048,8]{0,1:T(8,128)}, f32[2048,8]{0,1:T(8,128)S(1)}, u32[]{:S(2)}) copy-start(f32[2048,8]{0,1:T(8,128)S(1)} %get-tuple-element.258) | copy-start | bytes 196612
  37.7 201.7 %copy-start.29 = (f32[2048,8]{0,1:T(8,128)}, f32[2048,8]{0,1:T(8,128)S(1)}, u32[]{:S(2)}) copy-start(f32[2048,8]{0,1:T(8,128)S(1)} %get-tuple-element.257) | copy-start | bytes 196612
  100.2 10.9 %copy-start.22 = (bf16[2560,64]{1,0:T(8,128)(2,1)}, bf16[2560,64]{1,0:T(8,128)(2,1)S(1)}, u32[]{:S(2)}) copy-start(bf16[2560,64]{1,0:T(8,128)(2,1)S(1)} %get-tuple-element.534) | copy-start | bytes 983044
  100.3 10.9 %copy-start.58 = (s32[32,512]{1,0:T(8,128)}, s32[32,512]{1,0:T(8,128)S(1)}, u32[]{:S(2)}) copy-start(s32[32,512]{1,0:T(8,128)S(1)} %get-tuple-element.544) | copy-start | bytes 196612
  103.5 7.7 copy-start.61
  115.1 16.1 %copy-start.31 = (bf16[2048,64]{0,1:T(8,128)(2,1)}, bf16[2048,64]{0,1:T(8,128)(2,1)S(1)}, u32[]{:S(2)}) copy-start(bf16[2048,64]{0,1:T(8,128)(2,1)S(1)} %get-tuple-element.295) | copy-start | bytes 786436
  115.4 15.8 %copy-start.49 = (f32[2048]{0:T(1024)}, f32[2048]{0:T(1024)S(1)}, u32[]{:S(2)}) copy-start(f32[2048]{0:T(1024)S(1)} %broadcast_multiply_fusion.11) | copy-start | bytes 24580
  115.5 15.7 %copy-start.59 = (f32[2048]{0:T(1024)}, f32[2048]{0:T(1024)S(1)}, u32[]{:S(2)}) copy-start(f32[2048]{0:T(1024)S(1)} %add_rsqrt_fusion.3) | copy-start | bytes 24580
  115.8 6.6 copy-start.11
  117.8 8.7 %collective-permute-start.4 = (bf16[1,128,64]{1,2,0:T(8,128)(2,1)S(1)}, bf16[1,128,64]{1,2,0:T(8,128)(2,1)S(1)}, u32[]{:S(2)}, u32[]{:S(2)}) collective-permute-start(bf16[1,128,64]{1,2,0:T(8,128)(2,1)S(1)} %get-tuple-element.272), channel_id=1, source_target_pairs={{0,4},{4,8},{8,12},{12,16},{16,20},{20,24},{24,28},{1,5},{5,9},{9,... | collective-permute-start | bytes 49160 | tf_op jit(solution)/shard_map/ppermute | solution.py:16
  123.4 5.6 collective-permute-start.5
  124.7 4.3 collective-permute-start.6
  124.8 4.3 collective-permute-start.7
  232.2 5.8 copy-start.62
  400.6 8.1 %copy-start.14 = (bf16[2048,64]{0,1:T(8,128)(2,1)S(1)}, bf16[2048,64]{0,1:T(8,128)(2,1)}, u32[]{:S(2)}) copy-start(bf16[2048,64]{0,1:T(8,128)(2,1)} %copy-done.13) | copy-start | bytes 786436
  400.6 8.1 %copy-start.40 = (bf16[2048,64]{0,1:T(8,128)(2,1)S(1)}, bf16[2048,64]{0,1:T(8,128)(2,1)}, u32[]{:S(2)}) copy-start(bf16[2048,64]{0,1:T(8,128)(2,1)} %copy-done.39) | copy-start | bytes 786436
  400.6 8.9 %copy-start.12 = (bf16[2048,64]{0,1:T(8,128)(2,1)S(1)}, bf16[2048,64]{0,1:T(8,128)(2,1)}, u32[]{:S(2)}) copy-start(bf16[2048,64]{0,1:T(8,128)(2,1)} %copy-done.11) | copy-start | bytes 786436
  400.6 9.8 %copy-start.8 = (bf16[2048,8,64]{0,2,1:T(8,128)(2,1)S(1)}, bf16[2048,8,64]{0,2,1:T(8,128)(2,1)}, u32[]{:S(2)}) copy-start(bf16[2048,8,64]{0,2,1:T(8,128)(2,1)} %copy-done.7) | copy-start | bytes 6291460
  400.6 9.8 %copy-start.10 = (bf16[2048,8,64]{0,2,1:T(8,128)(2,1)S(1)}, bf16[2048,8,64]{0,2,1:T(8,128)(2,1)}, u32[]{:S(2)}) copy-start(bf16[2048,8,64]{0,2,1:T(8,128)(2,1)} %copy-done.9) | copy-start | bytes 6291460
  404.4 7.3 copy-start.17
  404.4 7.3 copy-start.19
  414.4 15.7 %collective-permute-start.8 = (bf16[1,128,64]{1,2,0:T(8,128)(2,1)}, bf16[1,128,64]{1,2,0:T(8,128)(2,1)S(1)}, u32[]{:S(2)}, u32[]{:S(2)}) collective-permute-start(bf16[1,128,64]{1,2,0:T(8,128)(2,1)} %get-tuple-element.251), channel_id=1, source_target_pairs={{0,4},{4,8},{8,12},{12,16},{16,20},{20,24},{24,28},{1,5},{5,9},{9,... | collective-permute-start | bytes 49160 | tf_op jit(solution)/shard_map/ppermute | solution.py:16
  419.1 11.1 %collective-permute-start.9 = (bf16[1,128,64]{1,2,0:T(8,128)(2,1)}, bf16[1,128,64]{1,2,0:T(8,128)(2,1)S(1)}, u32[]{:S(2)}, u32[]{:S(2)}) collective-permute-start(bf16[1,128,64]{1,2,0:T(8,128)(2,1)} %get-tuple-element.254), channel_id=1, source_target_pairs={{4,0},{8,4},{12,8},{16,12},{20,16},{24,20},{28,24},{5,1},{9,5},{13... | collective-permute-start | bytes 49160 | tf_op jit(solution)/shard_map/ppermute | solution.py:19
  420.4 9.4 %collective-permute-start.10 = (bf16[1,128,64]{1,2,0:T(8,128)(2,1)}, bf16[1,128,64]{1,2,0:T(8,128)(2,1)S(1)}, u32[]{:S(2)}, u32[]{:S(2)}) collective-permute-start(bf16[1,128,64]{1,2,0:T(8,128)(2,1)} %get-tuple-element.253), channel_id=1, source_target_pairs={{0,1},{1,2},{2,3},{3,0},{4,5},{5,6},{6,7},{7,4},{8,9},{9,10},{10,1... | collective-permute-start | bytes 49160 | tf_op jit(solution)/shard_map/ppermute | solution.py:16
  420.5 9.4 %collective-permute-start.11 = (bf16[1,128,64]{1,2,0:T(8,128)(2,1)}, bf16[1,128,64]{1,2,0:T(8,128)(2,1)S(1)}, u32[]{:S(2)}, u32[]{:S(2)}) collective-permute-start(bf16[1,128,64]{1,2,0:T(8,128)(2,1)} %get-tuple-element.252), channel_id=1, source_target_pairs={{1,0},{2,1},{3,2},{0,3},{5,4},{6,5},{7,6},{4,7},{9,8},{10,9},{11,1... | collective-permute-start | bytes 49160 | tf_op jit(solution)/shard_map/ppermute | solution.py:19
  423.0 5.0 copy-start.15
  423.0 5.0 copy-start.21
  423.0 5.0 copy-start.23
  423.0 5.0 copy-start.25
  423.1 5.0 copy-start.46
  423.1 5.3 copy-start.55
  423.1 6.0 copy-start.53
  423.1 6.0 copy-start.54
  423.1 6.7 copy-start.57
  423.1 6.7 copy-start.56
  423.1 7.0 copy-start.50
  423.1 7.0 copy-start.60
  423.1 7.0 copy-start.80
  423.2 7.0 copy-start.89
  428.1 5.9 copy-start.32
  428.1 6.7 copy-start.66
  430.2 6.6 copy-start.38
  432.7 4.9 copy-start.26
  432.7 6.1 copy-start.1
  432.7 6.1 copy-start.28
  432.7 6.1 copy-start.70
  432.7 6.1 copy-start.74
  451.5 95.2 %copy-start.48 = (bf16[2,192,64]{1,2,0:T(8,128)(2,1)S(1)}, bf16[2,192,64]{1,2,0:T(8,128)(2,1)}, u32[]{:S(2)}) copy-start(bf16[2,192,64]{1,2,0:T(8,128)(2,1)} %param.33) | copy-start | bytes 147460
  544.4 6.5 copy-start.2
  550.8 14.4 %copy-start.24 = (f32[2560,64]{0,1:T(8,128)S(1)}, f32[2560,64]{0,1:T(8,128)}, u32[]{:S(2)}) copy-start(f32[2560,64]{0,1:T(8,128)} %get-tuple-element.311) | copy-start | bytes 1966084
  557.6 14.0 %collective-permute-start.12 = (bf16[1,128,64]{1,2,0:T(8,128)(2,1)}, bf16[1,128,64]{1,2,0:T(8,128)(2,1)S(1)}, u32[]{:S(2)}, u32[]{:S(2)}) collective-permute-start(bf16[1,128,64]{1,2,0:T(8,128)(2,1)} %get-tuple-element.245), channel_id=1, source_target_pairs={{0,4},{4,8},{8,12},{12,16},{16,20},{20,24},{24,28},{1,5},{5,9},{9,... | collective-permute-start | bytes 49160 | tf_op jit(solution)/shard_map/ppermute | solution.py:16
  562.2 9.4 %collective-permute-start.13 = (bf16[1,128,64]{1,2,0:T(8,128)(2,1)S(1)}, bf16[1,128,64]{1,2,0:T(8,128)(2,1)S(1)}, u32[]{:S(2)}, u32[]{:S(2)}) collective-permute-start(bf16[1,128,64]{1,2,0:T(8,128)(2,1)S(1)} %get-tuple-element.248), channel_id=1, source_target_pairs={{4,0},{8,4},{12,8},{16,12},{20,16},{24,20},{28,24},{5,1},{9,5},{13... | collective-permute-start | bytes 49160 | tf_op jit(solution)/shard_map/ppermute | solution.py:19
  563.5 7.8 %collective-permute-start.14 = (bf16[1,128,64]{1,2,0:T(8,128)(2,1)}, bf16[1,128,64]{1,2,0:T(8,128)(2,1)S(1)}, u32[]{:S(2)}, u32[]{:S(2)}) collective-permute-start(bf16[1,128,64]{1,2,0:T(8,128)(2,1)} %get-tuple-element.247), channel_id=1, source_target_pairs={{0,1},{1,2},{2,3},{3,0},{4,5},{5,6},{6,7},{7,4},{8,9},{9,10},{10,1... | collective-permute-start | bytes 49160 | tf_op jit(solution)/shard_map/ppermute | solution.py:16
  563.5 7.8 %collective-permute-start.15 = (bf16[1,128,64]{1,2,0:T(8,128)(2,1)}, bf16[1,128,64]{1,2,0:T(8,128)(2,1)S(1)}, u32[]{:S(2)}, u32[]{:S(2)}) collective-permute-start(bf16[1,128,64]{1,2,0:T(8,128)(2,1)} %get-tuple-element.246), channel_id=1, source_target_pairs={{1,0},{2,1},{3,2},{0,3},{5,4},{6,5},{7,6},{4,7},{9,8},{10,9},{11,1... | collective-permute-start | bytes 49160 | tf_op jit(solution)/shard_map/ppermute | solution.py:19
  (44 other events, 113.6 us)
Sparse Core Ops, SparseCore 0:
  571.4 187.2 all-reduce.2
where the time goes:
time: 793 us; the launch traced here: 779 us
  matrix products  367 us (46%)
  waiting for transfers between devices  186 us (23%)
  local copies, waits for them, and re-layouts  141 us (18%)
  other arithmetic  33.1 us (4%)
  starting transfers between devices  31.6 us (4%)
  between operations  16.7 us (2%)
    psum x1, waiting for transfers between devices, reduce_layer(): return lax.psum(grads, ('band', 'lon'))  184 us
    dot_general x102, matrix products, matmul(): return jnp.dot(left, right, preferred_element_type=jnp.float32)  182 us
    dot_general x64, matrix products, add_block(): lax.dot_general(selector, block_values, (((0,), (0,)), ((), ())), preferr...  173 us
    dynamic_slice x128, local copies, waits for them, and re-layouts, gather_rows(): picked = lax.map(pick_block, blocks)  88.4 us
    ppermute x8, starting transfers between devices, extended(): lax.ppermute(lax.slice_in_dim(block, block.shape[dim] - width, None, axis...  19.5 us
    another operation x14, other arithmetic, shards(): jnp.stack([first, second])  17.4 us
  transfers between devices with their start and end apart: 17, of which 2 were waited for; matrix products, arithmetic and copies ran while one was open for 7% of the time, Pallas kernels for 0%

commit v1 on v0

v1 whole, which is shorter than its diff:
```python
import functools
import types

import jax
import jax.numpy as jnp
from jax import lax
from jax.experimental import pallas as pl
from jax.experimental.pallas import tpu as pltpu
from jax.sharding import PartitionSpec as P

F32 = jnp.float32
BF16 = jnp.bfloat16
MESH = pl.DeviceIdType.MESH
LISTED = 1024
TILE = 256
GROUP = 4
EB1, EGAIN, ESHIFT, NB1, NGAIN, NSHIFT, CMASK = range(7)


def dot(left, right):
    return jnp.dot(left, right, preferred_element_type=F32)


def dot_nt(left, right):
    return lax.dot_general(left, right, (((1,), (1,)), ((), ())), preferred_element_type=F32)


def exact_dot(left, right, dims):
    return lax.dot_general(
        left, right, (dims, ((), ())), precision=lax.Precision.HIGHEST, preferred_element_type=F32
    )


def eye(size, kind):
    row = lax.broadcasted_iota(jnp.int32, (size, size), 0)
    col = lax.broadcasted_iota(jnp.int32, (size, size), 1)
    return (row == col).astype(F32).astype(kind)


def turned(matrix):
    return dot_nt(eye(matrix.shape[1], BF16), matrix).astype(BF16)


def one_hot(row, total):
    width = row.shape[1]
    index = lax.broadcasted_iota(jnp.int16, (total, width), 0)
    return jnp.where(
        index == jnp.broadcast_to(row.astype(jnp.int16), (total, width)), BF16(1), BF16(0)
    )


def join(parts):
    return parts[0] if len(parts) == 1 else jnp.concatenate(parts, axis=1)


def mean0(values):
    return jnp.mean(values, axis=0, keepdims=True)


def gate(half):
    bend = jnp.tanh(half)
    act = half + half * bend
    return act, (1.0 + bend) + act * (1.0 - bend)


def fold(values):
    total = values[:, :128]
    for at in range(128, values.shape[1], 128):
        total = total + values[:, at : at + 128]
    return total


def kernel(names, bands, lons, *refs):
    k = types.SimpleNamespace(**dict(zip(names, refs)))
    band, lon = lax.axis_index("band"), lax.axis_index("lon")
    wide, nodes = k.state.shape
    degree = k.nbr.shape[1]
    halo = k.lists.shape[1]
    high = 4 * halo
    locals_ = nodes // high
    parts = locals_ + 1
    count = k.count[0]
    west, east = lax.rem(lon + lons - 1, lons), lax.rem(lon + 1, lons)
    has_low, has_high = band > 0, band < bands - 1

    for use in range(2):
        for way in range(2):
            k.halos[use, way] = jnp.zeros((wide, halo), BF16)
            k.backs[use, way] = jnp.zeros((wide, halo), BF16)
    barrier = pltpu.get_barrier_semaphore()

    def greet_band(step, carry):
        other = lax.rem(band + step, bands)
        pl.semaphore_signal(barrier, inc=1, device_id=(other, lon), device_id_type=MESH)
        return carry

    def greet_lon(step, carry):
        other = lax.rem(lon + step, lons)
        pl.semaphore_signal(barrier, inc=1, device_id=(band, other), device_id_type=MESH)
        return carry

    lax.fori_loop(1, bands, greet_band, 0)
    lax.fori_loop(1, lons, greet_lon, 0)

    def exchange(source, target, sends, recvs, use):
        def copy(block, landing, device):
            return pltpu.make_async_remote_copy(
                src_ref=source.at[use, block],
                dst_ref=target.at[use, landing],
                send_sem=sends.at[use, block],
                recv_sem=recvs.at[use, landing],
                device_id=device,
                device_id_type=MESH,
            )

        return copy

    turn = (1, 0, 3, 2)

    def targets():
        return ((band - 1, lon), (band + 1, lon), (band, west), (band, east))

    def start_exchange(copy):
        peers = targets()
        for block in range(4):
            go = copy(block, turn[block], peers[block]).start
            if block == 0:
                pl.when(has_low)(go)
            elif block == 1:
                pl.when(has_high)(go)
            else:
                go()

    def finish_exchange(copy):
        peers = targets()
        for block in range(4):
            def end(block=block):
                copy(block, block, peers[block]).wait()

            if block == 0:
                pl.when(has_low)(end)
            elif block == 1:
                pl.when(has_high)(end)
            else:
                end()

    for at, rows in enumerate((k.eb1, k.egain, k.eshift, k.nb1, k.ngain, k.nshift)):
        k.vrows[2 * at : 2 * at + 2, :] = rows[...]
    k.vrows[12:14, :] = k.cmask[...].astype(F32)
    k.vrows[14:16, :] = jnp.zeros((2, wide), F32)
    k.cols[...] = exact_dot(eye(wide, F32), k.vrows[...], ((1,), (1,)))

    def col(layer, which):
        at = 2 * which + layer
        return k.cols[:, at : at + 1]

    for way in range(4):
        k.owner[:, way * halo : (way + 1) * halo] = one_hot(k.lists[way : way + 1, :], LISTED)

    weights = []
    for layer in range(2):
        w1t = k.ew1t[layer]
        n1t = k.nw1t[layer]
        w2 = k.ew2[layer]
        n2 = k.nw2[layer]
        half = BF16(0.5)
        weights.append(
            dict(
                sender=w1t[:, :wide] * half,
                receiver=w1t[:, wide : 2 * wide] * half,
                attr=w1t[:, 2 * wide :] * half,
                second=turned(w2),
                node_one=n1t * half,
                node_two=turned(n2),
                sender_back=turned(w1t[:, :wide]),
                receiver_back=turned(w1t[:, wide : 2 * wide]),
                second_back=w2 * half,
                node_one_back=turned(n1t),
                node_two_back=n2 * half,
            )
        )
    for layer in range(2):
        for at, name in enumerate(
            (
                "sender", "receiver", "attr", "second", "node_two",
                "sender_back", "receiver_back", "second_back", "node_two_back",
            )
        ):
            k.small[layer, at] = weights[layer][name]
        k.wide_w[layer] = weights[layer]["node_one"]
        k.tall_w[layer] = weights[layer]["node_one_back"]
    SENDER, RECEIVER, ATTR, SECOND, NODE_TWO, SENDER_B, RECEIVER_B, SECOND_B, NODE_TWO_B = range(9)

    band_low_ok = has_low
    band_high_ok = has_high

    def tile_index(layer, at):
        lanes = pl.ds(pl.multiple_of(at * TILE, TILE), TILE)
        index = k.nbr[layer, :, lanes]
        place = lax.broadcasted_iota(jnp.int32, (1, TILE), 1) + at * TILE
        live = place < count
        return lanes, index, live

    def forward(layer):
        low = k.xs[layer, :wide, :]
        picked = dot(low[:, :LISTED], k.owner[...]).astype(BF16)
        for way in range(4):
            k.sends[layer, way] = picked[:, way * halo : (way + 1) * halo]
        copy = exchange(k.sends, k.halos, k.halo_send, k.halo_recv, layer)
        if layer == 0:
            pl.semaphore_wait(barrier, bands + lons - 2)
        start_exchange(copy)
        k.base[...] = dot(k.small[layer, RECEIVER], low) + 0.5 * col(layer, EB1)
        projected = dot(k.small[layer, SENDER], low).astype(BF16)
        for part in range(locals_):
            k.table[part * wide : (part + 1) * wide, :] = projected[
                :, part * high : (part + 1) * high
            ]
        finish_exchange(copy)
        for way in range(4):
            k.table[locals_ * wide :, way * halo : (way + 1) * halo] = dot(
                k.small[layer, SENDER], k.halos[layer, way]
            ).astype(BF16)

        def body(at, carry):
            lanes, index, live = tile_index(layer, at)
            sub, hi = index // high, index % high
            sender_ok = jnp.where(
                index < nodes,
                (index < count).astype(F32),
                jnp.where(
                    index < nodes + halo,
                    band_low_ok.astype(F32),
                    jnp.where(index < nodes + 2 * halo, band_high_ok.astype(F32), 1.0),
                ),
            )
            valid = live.astype(F32)
            edge_ok = sender_ok * valid
            base = k.base[:, lanes].reshape(wide // 8, 8, TILE)
            total = jnp.zeros((wide, TILE), F32)
            for first in range(0, degree, GROUP):
                slots = range(first, first + GROUP)
                hot = join([one_hot(hi[j : j + 1], high) for j in slots])
                found = dot(k.table[...], hot)
                for place, j in enumerate(slots):
                    piece = found[:, place * TILE : (place + 1) * TILE]
                    piece = piece.reshape(parts, wide // 8, 8, TILE)
                    which = jnp.broadcast_to(sub[j : j + 1], (8, TILE))
                    chosen = piece[0]
                    for part in range(1, parts):
                        chosen = jnp.where((which == part)[None], piece[part], chosen)
                    own = dot(k.small[layer, ATTR], k.attr[layer, j, :, lanes])
                    half = (chosen + base).reshape(wide, TILE) + own
                    act, slope = gate(half)
                    act = act.astype(BF16)
                    k.act[layer, j, :, lanes] = act
                    k.slope[layer, j, :, lanes] = slope.astype(BF16)
                    second = dot(k.small[layer, SECOND], act)
                    center = second - mean0(second)
                    rate = lax.rsqrt(mean0(center * center) + 1e-05) * edge_ok[j : j + 1]
                    k.rate_e[layer, j : j + 1, lanes] = rate
                    unit = center * rate
                    k.unit[layer, j, :, lanes] = unit.astype(BF16)
                    total = total + unit
            kept = jnp.sum(edge_ok, axis=0, keepdims=True)
            k.total[layer, :, lanes] = total
            k.kept[layer, :, lanes] = kept
            mask = col(layer, CMASK)
            summed = (mask * col(layer, EGAIN)) * total + (mask * col(layer, ESHIFT)) * kept
            k.xs[layer, wide:, lanes] = summed.astype(BF16)
            half = dot(k.wide_w[layer], k.xs[layer, :, lanes]) + 0.5 * col(layer, NB1)
            act, slope = gate(half)
            act = act.astype(BF16)
            k.act_n[layer, :, lanes] = act
            k.slope_n[layer, :, lanes] = slope.astype(BF16)
            fourth = dot(k.small[layer, NODE_TWO], act)
            center = fourth - mean0(fourth)
            rate = lax.rsqrt(mean0(center * center) + 1e-05)
            unit = center * rate
            k.rate_n[layer, :, lanes] = rate
            k.unit_n[layer, :, lanes] = unit
            change = valid * (unit * col(layer, NGAIN) + col(layer, NSHIFT))
            if layer == 0:
                middle = k.state[:, lanes].astype(F32) + change + k.latent[:, lanes].astype(F32)
                k.middle[:, lanes] = middle
                k.xs[1, :wide, lanes] = middle.astype(BF16)
            else:
                k.mesh_out[:, lanes] = (k.middle[:, lanes] + change).astype(BF16)
            return carry

        lax.fori_loop(0, nodes // TILE, body, 0)

    def backward(layer):
        into = k.grad_latent if layer == 1 else k.grad_state
        k.scatter[...] = jnp.zeros_like(k.scatter)
        k.sums[...] = jnp.zeros_like(k.sums)
        k.acc_64[...] = jnp.zeros_like(k.acc_64)
        k.acc_128[...] = jnp.zeros_like(k.acc_128)

        def body(at, carry):
            lanes, index, live = tile_index(layer, at)
            sub, hi = index // high, index % high
            valid = live.astype(F32)
            if layer == 1:
                grad = k.out_grad[:, lanes].astype(F32)
            else:
                grad = k.grad_latent[:, lanes]
            unit = k.unit_n[layer, :, lanes]
            grad_ok = valid * grad
            k.sums[NGAIN] += fold(grad_ok * unit)
            k.sums[NSHIFT] += fold(grad_ok)
            scaled = grad_ok * col(layer, NGAIN)
            fourth = k.rate_n[layer, :, lanes] * (
                scaled - mean0(scaled) - unit * mean0(scaled * unit)
            )
            fourth = fourth.astype(BF16)
            node_two = dot_nt(k.act_n[layer, :, lanes], fourth)
            third = dot(k.small[layer, NODE_TWO_B], fourth) * k.slope_n[layer, :, lanes].astype(F32)
            k.sums[NB1] += fold(third)
            third = third.astype(BF16)
            k.acc_128[...] += dot_nt(third, k.xs[layer, :, lanes])
            both = dot(k.tall_w[layer], third)
            state = grad + both[:wide]
            masked = both[wide:] * col(layer, CMASK)
            k.sums[EGAIN] += fold(masked * k.total[layer, :, lanes])
            k.sums[ESHIFT] += fold(masked * k.kept[layer, :, lanes])
            scaled = masked * col(layer, EGAIN)
            middle = scaled - mean0(scaled)
            first_sum = jnp.zeros((wide, TILE), F32)
            grad_two = jnp.zeros((wide, wide), F32)
            grad_attr = jnp.zeros((wide, wide), F32)
            for first in range(0, degree, GROUP):
                slots = range(first, first + GROUP)
                hots, spreads, seconds, firsts = [], [], [], []
                for j in slots:
                    unit = k.unit[layer, j, :, lanes].astype(F32)
                    second = (middle - unit * mean0(scaled * unit)) * k.rate_e[
                        layer, j : j + 1, lanes
                    ]
                    second = second.astype(BF16)
                    grad_one = dot(k.small[layer, SECOND_B], second) * k.slope[
                        layer, j, :, lanes
                    ].astype(F32)
                    first_sum = first_sum + grad_one
                    grad_one = grad_one.astype(BF16)
                    which = jnp.broadcast_to(sub[j : j + 1].astype(jnp.int16), (16, TILE))
                    rows = grad_one.reshape(wide // 16, 16, TILE)
                    spreads.append(
                        jnp.concatenate(
                            [
                                jnp.where((which == part)[None], rows, BF16(0)).reshape(wide, TILE)
                                for part in range(parts)
                            ],
                            axis=0,
                        )
                    )
                    hots.append(one_hot(hi[j : j + 1], high))
                    seconds.append(second)
                    firsts.append(grad_one)
                k.scatter[...] += dot_nt(join(spreads), join(hots))
                grad_two = grad_two + dot_nt(
                    join([k.act[layer, j, :, lanes] for j in slots]), join(seconds)
                )
                grad_attr = grad_attr + dot_nt(
                    join(firsts), join([k.attr[layer, j, :, lanes] for j in slots])
                )
            k.sums[EB1] += fold(first_sum)
            first_sum = first_sum.astype(BF16)
            k.acc_64[0] += dot_nt(first_sum, k.xs[layer, :wide, lanes])
            k.acc_64[1] += grad_attr
            k.acc_64[2] += grad_two
            k.acc_64[3] += node_two
            into[:, lanes] = state + dot(k.small[layer, RECEIVER_B], first_sum)
            return carry

        lax.fori_loop(0, nodes // TILE, body, 0)

        summed = k.scatter[...]
        coarse = summed.astype(BF16)
        fine = (summed - coarse.astype(F32)).astype(BF16)
        back = k.small[layer, SENDER_B]
        last = slice(locals_ * wide, parts * wide)
        to_owner = (dot(back, coarse[last]) + dot(back, fine[last])).astype(BF16)
        for way in range(4):
            k.gives[layer, way] = to_owner[:, way * halo : (way + 1) * halo]
        copy = exchange(k.gives, k.backs, k.back_send, k.back_recv, layer)
        start_exchange(copy)

        halo_rows = join([k.halos[layer, way] for way in range(4)])
        sender = dot_nt(coarse[last], halo_rows) + dot_nt(fine[last], halo_rows)
        for part in range(locals_):
            span = slice(part * wide, (part + 1) * wide)
            place = slice(part * high, (part + 1) * high)
            rows = k.xs[layer, :wide, place]
            sender = sender + dot_nt(coarse[span], rows) + dot_nt(fine[span], rows)
            into[:, place] += dot(back, coarse[span]) + dot(back, fine[span])
        lane = lax.broadcasted_iota(jnp.int32, (wide, wide), 1)
        vectors = jnp.zeros((wide, wide), F32)
        for which in range(6):
            vectors = jnp.where(
                lane == which, jnp.sum(k.sums[which], axis=1, keepdims=True), vectors
            )
        blocks = (
            join([sender, k.acc_64[0]]),
            join([k.acc_64[1], k.acc_64[2]]),
            k.acc_128[...],
            join([k.acc_64[3], vectors]),
        )
        rows = k.share.shape[2]
        for at, block in enumerate(blocks):
            for piece in range(wide // rows):
                k.share[layer, at * (wide // rows) + piece] = block[
                    piece * rows : (piece + 1) * rows, :
                ]

        finish_exchange(copy)
        returned = join([k.backs[layer, way] for way in range(4)])
        into[:, :LISTED] += dot_nt(returned, k.owner[...])

    def reduce_layer(layer):
        def band_copy(source, landing, sends, recvs, piece, slot, other):
            return pltpu.make_async_remote_copy(
                src_ref=source.at[layer, piece],
                dst_ref=landing.at[layer, slot],
                send_sem=sends.at[layer, other],
                recv_sem=recvs.at[layer, slot],
                device_id=(other, lon),
                device_id_type=MESH,
            )

        def scatter_start(step, carry):
            other = lax.rem(band + step, bands)
            band_copy(k.share, k.spread, k.rs_send, k.rs_recv, other, band, other).start()
            return carry

        def scatter_end(step, carry):
            other = lax.rem(band + step, bands)
            band_copy(k.share, k.spread, k.rs_send, k.rs_recv, other, other, other).wait()
            return carry

        lax.fori_loop(1, bands, scatter_start, 0)
        k.spread[layer, band] = k.share[layer, band]
        lax.fori_loop(1, bands, scatter_end, 0)
        k.swap[layer, lon] = jnp.sum(k.spread[layer], axis=0)

        def lon_copy(slot, other):
            return pltpu.make_async_remote_copy(
                src_ref=k.swap.at[layer, lon],
                dst_ref=k.swap.at[layer, slot],
                send_sem=k.sw_send.at[layer, other],
                recv_sem=k.sw_recv.at[layer, slot],
                device_id=(band, other),
                device_id_type=MESH,
            )

        def swap_start(step, carry):
            lon_copy(lon, lax.rem(lon + step, lons)).start()
            return carry

        def swap_end(step, carry):
            other = lax.rem(lon + step, lons)
            lon_copy(other, other).wait()
            return carry

        lax.fori_loop(1, lons, swap_start, 0)
        lax.fori_loop(1, lons, swap_end, 0)
        k.whole[layer, band] = jnp.sum(k.swap[layer], axis=0)

        def gather_start(step, carry):
            other = lax.rem(band + step, bands)
            band_copy(k.whole, k.whole, k.ag_send, k.ag_recv, band, band, other).start()
            return carry

        def gather_end(step, carry):
            other = lax.rem(band + step, bands)
            band_copy(k.whole, k.whole, k.ag_send, k.ag_recv, band, other, other).wait()
            return carry

        lax.fori_loop(1, bands, gather_start, 0)
        lax.fori_loop(1, bands, gather_end, 0)

        rows = k.share.shape[2]
        pieces = wide // rows
        blocks = []
        for at in range(4):
            block = [k.whole[layer, at * pieces + piece] for piece in range(pieces)]
            blocks.append(block[0] if pieces == 1 else jnp.concatenate(block, axis=0))
        k.g_ew1t[layer, :, : 2 * wide] = blocks[0]
        k.g_ew1t[layer, :, 2 * wide :] = blocks[1][:, :wide]
        k.g_ew2[layer] = blocks[1][:, wide:]
        k.g_nw1t[layer] = blocks[2]
        k.g_nw2[layer] = blocks[3][:, :wide]
        lines = exact_dot(blocks[3][:, wide:], eye(wide, F32), ((0,), (0,)))
        for which, out in enumerate(
            (k.g_eb1, k.g_egain, k.g_eshift, k.g_nb1, k.g_ngain, k.g_nshift)
        ):
            out[layer : layer + 1, :] = lines[which : which + 1, :]

    k.xs[0, :wide, :] = k.state[...]
    forward(0)
    forward(1)
    backward(1)
    backward(0)
    reduce_layer(1)
    reduce_layer(0)


INPUTS = (
    "state", "latent", "attr", "nbr", "lists", "count", "cmask", "ew1t", "eb1", "ew2",
    "egain", "eshift", "nw1t", "nb1", "nw2", "ngain", "nshift", "out_grad",
)
OUTPUTS = (
    "mesh_out", "grad_state", "grad_latent", "g_ew1t", "g_eb1", "g_ew2", "g_egain",
    "g_eshift", "g_nw1t", "g_nb1", "g_nw2", "g_ngain", "g_nshift",
)


def shards(bands, lons, *args):
    (
        node_state, latent, edge_attr, neighbours, halo_lists, valid_counts, channel_mask,
        edge_w1, edge_b1, edge_w2, edge_gain, edge_shift,
        node_w1, node_b1, node_w2, node_gain, node_shift, out_grad,
    ) = args
    nodes, wide = node_state.shape
    degree = neighbours.shape[2]
    halo = halo_lists.shape[1]
    high = 4 * halo
    parts = nodes // high + 1
    rows = max(8, 4 * wide // bands)
    while wide % rows:
        rows //= 2
    pieces = max(bands, 4 * wide // rows)
    shape = jax.ShapeDtypeStruct
    outs = (
        shape((wide, nodes), BF16),
        shape((wide, nodes), F32),
        shape((wide, nodes), F32),
        shape((2, wide, 3 * wide), F32),
        shape((2, wide), F32),
        shape((2, wide, wide), F32),
        shape((2, wide), F32),
        shape((2, wide), F32),
        shape((2, wide, 2 * wide), F32),
        shape((2, wide), F32),
        shape((2, wide, wide), F32),
        shape((2, wide), F32),
        shape((2, wide), F32),
    )
    sem = pltpu.SemaphoreType.DMA
    scratch = dict(
        halos=pltpu.VMEM((2, 4, wide, halo), BF16),
        backs=pltpu.VMEM((2, 4, wide, halo), BF16),
        sends=pltpu.VMEM((2, 4, wide, halo), BF16),
        gives=pltpu.VMEM((2, 4, wide, halo), BF16),
        share=pltpu.VMEM((2, pieces, rows, 128), F32),
        spread=pltpu.VMEM((2, bands, rows, 128), F32),
        swap=pltpu.VMEM((2, lons, rows, 128), F32),
        whole=pltpu.VMEM((2, pieces, rows, 128), F32),
        vrows=pltpu.VMEM((16, wide), F32),
        cols=pltpu.VMEM((wide, 16), F32),
        owner=pltpu.VMEM((LISTED, high), BF16),
        small=pltpu.VMEM((2, 9, wide, wide), BF16),
        wide_w=pltpu.VMEM((2, wide, 2 * wide), BF16),
        tall_w=pltpu.VMEM((2, 2 * wide, wide), BF16),
        xs=pltpu.VMEM((2, 2 * wide, nodes), BF16),
        base=pltpu.VMEM((wide, nodes), F32),
        table=pltpu.VMEM((parts * wide, high), BF16),
        act=pltpu.VMEM((2, degree, wide, nodes), BF16),
        slope=pltpu.VMEM((2, degree, wide, nodes), BF16),
        unit=pltpu.VMEM((2, degree, wide, nodes), BF16),
        rate_e=pltpu.VMEM((2, degree, nodes), F32),
        total=pltpu.VMEM((2, wide, nodes), F32),
        kept=pltpu.VMEM((2, 1, nodes), F32),
        act_n=pltpu.VMEM((2, wide, nodes), BF16),
        slope_n=pltpu.VMEM((2, wide, nodes), BF16),
        rate_n=pltpu.VMEM((2, 1, nodes), F32),
        unit_n=pltpu.VMEM((2, wide, nodes), F32),
        middle=pltpu.VMEM((wide, nodes), F32),
        scatter=pltpu.VMEM((parts * wide, high), F32),
        sums=pltpu.VMEM((6, wide, 128), F32),
        acc_64=pltpu.VMEM((4, wide, wide), F32),
        acc_128=pltpu.VMEM((wide, 2 * wide), F32),
        halo_send=sem((2, 4)),
        halo_recv=sem((2, 4)),
        back_send=sem((2, 4)),
        back_recv=sem((2, 4)),
        rs_send=sem((2, bands)),
        rs_recv=sem((2, bands)),
        sw_send=sem((2, lons)),
        sw_recv=sem((2, lons)),
        ag_send=sem((2, bands)),
        ag_recv=sem((2, bands)),
    )
    vmem = pl.BlockSpec(memory_space=pltpu.VMEM)
    specs = [vmem] * len(INPUTS)
    specs[INPUTS.index("count")] = pl.BlockSpec(memory_space=pltpu.SMEM)
    names = INPUTS + OUTPUTS + tuple(scratch)
    result = pl.pallas_call(
        functools.partial(kernel, names, bands, lons),
        out_shape=outs,
        in_specs=specs,
        out_specs=(vmem,) * len(OUTPUTS),
        scratch_shapes=list(scratch.values()),
        compiler_params=pltpu.CompilerParams(
            collective_id=0, has_side_effects=True, vmem_limit_bytes=60 * 2**20
        ),
        name="layers",
    )(
        node_state.T,
        latent.T,
        edge_attr.transpose(0, 2, 3, 1),
        neighbours.transpose(0, 2, 1),
        halo_lists,
        valid_counts,
        channel_mask,
        edge_w1.transpose(0, 2, 1),
        edge_b1,
        edge_w2,
        edge_gain,
        edge_shift,
        node_w1.transpose(0, 2, 1),
        node_b1,
        node_w2,
        node_gain,
        node_shift,
        out_grad.T,
    )
    result = list(result)
    for at in range(3):
        result[at] = result[at].T
    for at in (3, 8):
        result[at] = result[at].transpose(0, 2, 1)
    return tuple(result)


def solution(mesh):
    nodes = P(("band", "lon"), None)
    whole = P()
    in_specs = (
        nodes,
        nodes,
        P(None, ("band", "lon"), None, None),
        P(None, ("band", "lon"), None),
        nodes,
        P(("band", "lon")),
    ) + (whole,) * 11 + (nodes,)
    return jax.shard_map(
        functools.partial(shards, mesh.shape["band"], mesh.shape["lon"]),
        mesh=mesh,
        in_specs=in_specs,
        out_specs=(nodes,) * 3 + (whole,) * 10,
        check_vma=False,
    )
```

time: 793 us -> 125 us (0.16); the launches traced: 779 us -> 124 us
  matrix products: 367 us -> 0 us
  waiting for transfers between devices: 186 us -> 0 us
  local copies, waits for them, and re-layouts: 141 us -> 18.8 us
  Pallas kernels: 0 us -> 104 us
  other arithmetic: 33.1 us -> 0 us
  starting transfers between devices: 31.6 us -> 0 us
  between operations: 16.7 us -> 1.31 us
    dot_general x172 -> x0, matrix products: 367 us -> none  [the longest x102 182 us: matmul(): return jnp.dot(left, right, preferred_element_type=jnp.float32)]
    psum x1 -> x0, waiting for transfers between devices: 184 us -> none  [reduce_layer(): return lax.psum(grads, ('band', 'lon'))]
    pallas_call x0 -> x1, Pallas kernels: none -> 104 us  [shards(): pl.pallas_call(functools.partial(kernel, names, bands, lons), out_shape=o...]
    dynamic_slice x128 -> x0, local copies, waits for them, and re-layouts: 88.4 us -> none  [gather_rows(): picked = lax.map(pick_block, blocks)]
    ppermute x16 -> x0, starting transfers between devices: 31.5 us -> none  [the longest x8 19.5 us: extended(): lax.ppermute(lax.slice_in_dim(block, block.shape[dim] - width, None, axis...]
    another operation x14 -> x0, other arithmetic: 17.4 us -> none  [shards(): jnp.stack([first, second])]
    slice x10 -> x0, local copies, waits for them, and re-layouts: 16.7 us -> none  [the longest x3 12.2 us: layer_inputs(): return (params, neighbour, edge_attr[layer_at], scale)]
    unnamed x192 -> x13, local copies, waits for them, and re-layouts: 4.19 us -> 18.8 us
  transfers between devices with their start and end apart: 17 -> 0, of which waited for: 2 -> 0; matrix products, arithmetic and copies ran while one was open for 7% -> 0% of each run, Pallas kernels for 0% -> 0%
where the time goes in v1:
time: 125 us; the launch traced here: 124 us
  Pallas kernels  104 us (83%)
  local copies, waits for them, and re-layouts  18.8 us (15%)
  between operations  1.31 us (1%)
    pallas_call x1, Pallas kernels, shards(): pl.pallas_call(functools.partial(kernel, names, bands, lons), out_shape=o...  104 us
    unnamed x13, local copies, waits for them, and re-layouts  18.8 us

profile of v1, /device:TPU:0, one launch (start us, length us, event | category | flops | bytes accessed | tf_op | source)
XLA Modules:
  0.0 124.3 jit_solution(13208261304110941932)
XLA Ops:
  1.3 104.2 %layers.1 = (bf16[64,2048]{1,0:T(8,128)(2,1)}, f32[64,2048]{1,0:T(8,128)}, f32[64,2048]{1,0:T(8,128)}, f32[2,64,192]{2,1,0:T(8,128)}, f32[2,64]{1,0:T(2,128)}, /...) custom-call(bf16[64,2048]{1,0:T(8,128)(2,1)} %bitcast.15, ...), custom_call_target="tpu_custom_call" | custom-call | tf_op jit(solution)/shard_map/layers/pallas_call | solution.py:598
  105.5 1.7 %copy.45 = bf16[2048,64]{0,1:T(8,128)(2,1)} copy(bf16[2048,64]{0,1:T(8,128)(2,1)} %bitcast.18) | data formatting | bytes 524288
  107.2 1.9 %copy.46 = f32[2048,64]{0,1:T(8,128)} copy(f32[2048,64]{0,1:T(8,128)} %bitcast.14) | data formatting | bytes 1048576
  109.0 1.9 %copy.47 = f32[2048,64]{0,1:T(8,128)} copy(f32[2048,64]{0,1:T(8,128)} %bitcast.13) | data formatting | bytes 1048576
  110.9 1.6 %copy.48 = f32[2,192,64]{1,2,0:T(8,128)} copy(f32[2,192,64]{1,2,0:T(8,128)} %bitcast.20) | data formatting | bytes 196608
  112.5 1.2 %copy.49 = f32[2,64]{1,0:T(2,128)} copy(f32[2,64]{1,0:T(2,128)} %get-tuple-element.56) | data formatting | bytes 1024
  113.7 1.5 %copy.50 = f32[2,64,64]{2,1,0:T(8,128)} copy(f32[2,64,64]{2,1,0:T(8,128)} %get-tuple-element.57) | data formatting | bytes 65536
  115.2 1.2 copy.51
  116.4 1.2 copy.52
  117.6 1.5 %copy.53 = f32[2,128,64]{1,2,0:T(8,128)} copy(f32[2,128,64]{1,2,0:T(8,128)} %bitcast.22) | data formatting | bytes 131072
  119.1 1.2 copy.54
  120.4 1.5 %copy.55 = f32[2,64,64]{2,1,0:T(8,128)} copy(f32[2,64,64]{2,1,0:T(8,128)} %get-tuple-element.62) | data formatting | bytes 65536
  121.8 1.2 copy.56
  123.1 1.2 copy.57

commit v2 on v1

--- a/solution.py
+++ b/solution.py
@@ -14,6 +14,7 @@
 LISTED = 1024
 TILE = 256
 GROUP = 4
+CHUNK = 256
 EB1, EGAIN, ESHIFT, NB1, NGAIN, NSHIFT, CMASK = range(7)
 
 
@@ -77,6 +78,7 @@
     degree = k.nbr.shape[1]
     halo = k.lists.shape[1]
     high = 4 * halo
+    shift = high.bit_length() - 1
     locals_ = nodes // high
     parts = locals_ + 1
     count = k.count[0]
@@ -191,52 +193,54 @@
         k.tall_w[layer] = weights[layer]["node_one_back"]
     SENDER, RECEIVER, ATTR, SECOND, NODE_TWO, SENDER_B, RECEIVER_B, SECOND_B, NODE_TWO_B = range(9)
 
-    band_low_ok = has_low
-    band_high_ok = has_high
-
-    def tile_index(layer, at):
-        lanes = pl.ds(pl.multiple_of(at * TILE, TILE), TILE)
+    def split_index(layer, lanes):
         index = k.nbr[layer, :, lanes]
-        place = lax.broadcasted_iota(jnp.int32, (1, TILE), 1) + at * TILE
-        live = place < count
-        return lanes, index, live
-
-    def forward(layer):
-        low = k.xs[layer, :wide, :]
-        picked = dot(low[:, :LISTED], k.owner[...]).astype(BF16)
+        return index, index >> shift, index & (high - 1)
+
+    def live_lanes(start, width):
+        return lax.broadcasted_iota(jnp.int32, (1, width), 1) + start < count
+
+    def node_lanes(first, last):
+        return [pl.ds(at, CHUNK) for at in range(first, last, CHUNK)]
+
+    def send_halos(layer):
+        picked = dot(k.xs[layer, :wide, :LISTED], k.owner[...]).astype(BF16)
         for way in range(4):
             k.sends[layer, way] = picked[:, way * halo : (way + 1) * halo]
-        copy = exchange(k.sends, k.halos, k.halo_send, k.halo_recv, layer)
-        if layer == 0:
-            pl.semaphore_wait(barrier, bands + lons - 2)
-        start_exchange(copy)
+        start_exchange(exchange(k.sends, k.halos, k.halo_send, k.halo_recv, layer))
+
+    def project(layer):
+        low = k.xs[layer, :wide, :]
         k.base[...] = dot(k.small[layer, RECEIVER], low) + 0.5 * col(layer, EB1)
         projected = dot(k.small[layer, SENDER], low).astype(BF16)
         for part in range(locals_):
             k.table[part * wide : (part + 1) * wide, :] = projected[
                 :, part * high : (part + 1) * high
             ]
-        finish_exchange(copy)
+
+    def project_halos(layer):
+        finish_exchange(exchange(k.sends, k.halos, k.halo_send, k.halo_recv, layer))
         for way in range(4):
             k.table[locals_ * wide :, way * halo : (way + 1) * halo] = dot(
                 k.small[layer, SENDER], k.halos[layer, way]
             ).astype(BF16)
 
+    def edges_forward(layer):
         def body(at, carry):
-            lanes, index, live = tile_index(layer, at)
-            sub, hi = index // high, index % high
+            start = pl.multiple_of(at * TILE, TILE)
+            lanes = pl.ds(start, TILE)
+            index, sub, hi = split_index(layer, lanes)
             sender_ok = jnp.where(
                 index < nodes,
                 (index < count).astype(F32),
                 jnp.where(
                     index < nodes + halo,
-                    band_low_ok.astype(F32),
-                    jnp.where(index < nodes + 2 * halo, band_high_ok.astype(F32), 1.0),
+                    has_low.astype(F32),
+                    jnp.where(index < nodes + 2 * halo, has_high.astype(F32), 1.0),
                 ),
             )
-            valid = live.astype(F32)
-            edge_ok = sender_ok * valid
-            base = k.base[:, lanes].reshape(wide // 8, 8, TILE)
+            edge_ok = sender_ok * live_lanes(start, TILE).astype(F32)
+            base = k.base[:, lanes]
             total = jnp.zeros((wide, TILE), F32)
             for first in range(0, degree, GROUP):
                 slots = range(first, first + GROUP)
@@ -250,8 +254,7 @@
                     for part in range(1, parts):
                         chosen = jnp.where((which == part)[None], piece[part], chosen)
                     own = dot(k.small[layer, ATTR], k.attr[layer, j, :, lanes])
-                    half = (chosen + base).reshape(wide, TILE) + own
-                    act, slope = gate(half)
+                    act, slope = gate(chosen.reshape(wide, TILE) + base + own)
                     act = act.astype(BF16)
                     k.act[layer, j, :, lanes] = act
                     k.slope[layer, j, :, lanes] = slope.astype(BF16)
@@ -262,11 +265,18 @@
                     unit = center * rate
                     k.unit[layer, j, :, lanes] = unit.astype(BF16)
                     total = total + unit
-            kept = jnp.sum(edge_ok, axis=0, keepdims=True)
             k.total[layer, :, lanes] = total
-            k.kept[layer, :, lanes] = kept
+            k.kept[layer, :, lanes] = jnp.sum(edge_ok, axis=0, keepdims=True)
+            return carry
+
+        lax.fori_loop(0, nodes // TILE, body, 0)
+
+    def nodes_forward(layer, first, last):
+        for lanes in node_lanes(first, last):
             mask = col(layer, CMASK)
-            summed = (mask * col(layer, EGAIN)) * total + (mask * col(layer, ESHIFT)) * kept
+            summed = (mask * col(layer, EGAIN)) * k.total[layer, :, lanes] + (
+                mask * col(layer, ESHIFT)
+            ) * k.kept[layer, :, lanes]
             k.xs[layer, wide:, lanes] = summed.astype(BF16)
             half = dot(k.wide_w[layer], k.xs[layer, :, lanes]) + 0.5 * col(layer, NB1)
             act, slope = gate(half)
@@ -279,6 +289,7 @@
             unit = center * rate
             k.rate_n[layer, :, lanes] = rate
             k.unit_n[layer, :, lanes] = unit
+            valid = live_lanes(lanes.start, CHUNK).astype(F32)
             change = valid * (unit * col(layer, NGAIN) + col(layer, NSHIFT))
             if layer == 0:
                 middle = k.state[:, lanes].astype(F32) + change + k.latent[:, lanes].astype(F32)
@@ -286,46 +297,47 @@
                 k.xs[1, :wide, lanes] = middle.astype(BF16)
             else:
                 k.mesh_out[:, lanes] = (k.middle[:, lanes] + change).astype(BF16)
-            return carry
-
-        lax.fori_loop(0, nodes // TILE, body, 0)
-
-    def backward(layer):
-        into = k.grad_latent if layer == 1 else k.grad_state
-        k.scatter[...] = jnp.zeros_like(k.scatter)
-        k.sums[...] = jnp.zeros_like(k.sums)
-        k.acc_64[...] = jnp.zeros_like(k.acc_64)
-        k.acc_128[...] = jnp.zeros_like(k.acc_128)
-
-        def body(at, carry):
-            lanes, index, live = tile_index(layer, at)
-            sub, hi = index // high, index % high
-            valid = live.astype(F32)
+
+    def into(layer):
+        return k.grad_latent if layer == 1 else k.grad_state
+
+    def nodes_backward(layer, first, last):
+        for lanes in node_lanes(first, last):
+            valid = live_lanes(lanes.start, CHUNK).astype(F32)
             if layer == 1:
                 grad = k.out_grad[:, lanes].astype(F32)
             else:
                 grad = k.grad_latent[:, lanes]
             unit = k.unit_n[layer, :, lanes]
             grad_ok = valid * grad
-            k.sums[NGAIN] += fold(grad_ok * unit)
-            k.sums[NSHIFT] += fold(grad_ok)
+            k.sums[layer, NGAIN] += fold(grad_ok * unit)
+            k.sums[layer, NSHIFT] += fold(grad_ok)
             scaled = grad_ok * col(layer, NGAIN)
             fourth = k.rate_n[layer, :, lanes] * (
                 scaled - mean0(scaled) - unit * mean0(scaled * unit)
             )
             fourth = fourth.astype(BF16)
-            node_two = dot_nt(k.act_n[layer, :, lanes], fourth)
+            k.acc_64[layer, 3] += dot_nt(k.act_n[layer, :, lanes], fourth)
             third = dot(k.small[layer, NODE_TWO_B], fourth) * k.slope_n[layer, :, lanes].astype(F32)
-            k.sums[NB1] += fold(third)
+            k.sums[layer, NB1] += fold(third)
             third = third.astype(BF16)
-            k.acc_128[...] += dot_nt(third, k.xs[layer, :, lanes])
+            k.acc_128[layer] += dot_nt(third, k.xs[layer, :, lanes])
             both = dot(k.tall_w[layer], third)
-            state = grad + both[:wide]
+            into(layer)[:, lanes] = grad + both[:wide]
             masked = both[wide:] * col(layer, CMASK)
-            k.sums[EGAIN] += fold(masked * k.total[layer, :, lanes])
-            k.sums[ESHIFT] += fold(masked * k.kept[layer, :, lanes])
+            k.sums[layer, EGAIN] += fold(masked * k.total[layer, :, lanes])
+            k.sums[layer, ESHIFT] += fold(masked * k.kept[layer, :, lanes])
             scaled = masked * col(layer, EGAIN)
-            middle = scaled - mean0(scaled)
+            k.scaled[:, lanes] = scaled
+            k.center[:, lanes] = scaled - mean0(scaled)
+
+    def edges_backward(layer):
+        k.scatter[...] = jnp.zeros_like(k.scatter)
+
+        def body(at, carry):
+            lanes = pl.ds(pl.multiple_of(at * TILE, TILE), TILE)
+            index, sub, hi = split_index(layer, lanes)
+            scaled, center = k.scaled[:, lanes], k.center[:, lanes]
             first_sum = jnp.zeros((wide, TILE), F32)
             grad_two = jnp.zeros((wide, wide), F32)
             grad_attr = jnp.zeros((wide, wide), F32)
@@ -334,7 +346,7 @@
                 hots, spreads, seconds, firsts = [], [], [], []
                 for j in slots:
                     unit = k.unit[layer, j, :, lanes].astype(F32)
-                    second = (middle - unit * mean0(scaled * unit)) * k.rate_e[
+                    second = (center - unit * mean0(scaled * unit)) * k.rate_e[
                         layer, j : j + 1, lanes
                     ]
                     second = second.astype(BF16)
@@ -364,17 +376,14 @@
                 grad_attr = grad_attr + dot_nt(
                     join(firsts), join([k.attr[layer, j, :, lanes] for j in slots])
                 )
-            k.sums[EB1] += fold(first_sum)
-            first_sum = first_sum.astype(BF16)
-            k.acc_64[0] += dot_nt(first_sum, k.xs[layer, :wide, lanes])
-            k.acc_64[1] += grad_attr
-            k.acc_64[2] += grad_two
-            k.acc_64[3] += node_two
-            into[:, lanes] = state + dot(k.small[layer, RECEIVER_B], first_sum)
+            k.first_sum[:, lanes] = first_sum
+            k.acc_64[layer, 1] += grad_attr
+            k.acc_64[layer, 2] += grad_two
             return carry
 
         lax.fori_loop(0, nodes // TILE, body, 0)
 
+    def give_back(layer):
         summed = k.scatter[...]
         coarse = summed.astype(BF16)
         fine = (summed - coarse.astype(F32)).astype(BF16)
@@ -383,28 +392,27 @@
         to_owner = (dot(back, coarse[last]) + dot(back, fine[last])).astype(BF16)
         for way in range(4):
             k.gives[layer, way] = to_owner[:, way * halo : (way + 1) * halo]
-        copy = exchange(k.gives, k.backs, k.back_send, k.back_recv, layer)
-        start_exchange(copy)
-
+        start_exchange(exchange(k.gives, k.backs, k.back_send, k.back_recv, layer))
+        k.sums[layer, EB1] = fold(k.first_sum[...])
+        first_sum = k.first_sum[...].astype(BF16)
+        receiver = dot_nt(first_sum, k.xs[layer, :wide, :])
         halo_rows = join([k.halos[layer, way] for way in range(4)])
         sender = dot_nt(coarse[last], halo_rows) + dot_nt(fine[last], halo_rows)
         for part in range(locals_):
             span = slice(part * wide, (part + 1) * wide)
-            place = slice(part * high, (part + 1) * high)
-            rows = k.xs[layer, :wide, place]
+            rows = k.xs[layer, :wide, part * high : (part + 1) * high]
             sender = sender + dot_nt(coarse[span], rows) + dot_nt(fine[span], rows)
-            into[:, place] += dot(back, coarse[span]) + dot(back, fine[span])
         lane = lax.broadcasted_iota(jnp.int32, (wide, wide), 1)
         vectors = jnp.zeros((wide, wide), F32)
         for which in range(6):
             vectors = jnp.where(
-                lane == which, jnp.sum(k.sums[which], axis=1, keepdims=True), vectors
+                lane == which, jnp.sum(k.sums[layer, which], axis=1, keepdims=True), vectors
             )
         blocks = (
-            join([sender, k.acc_64[0]]),
-            join([k.acc_64[1], k.acc_64[2]]),
-            k.acc_128[...],
-            join([k.acc_64[3], vectors]),
+            join([sender, receiver]),
+            join([k.acc_64[layer, 1], k.acc_64[layer, 2]]),
+            k.acc_128[layer],
+            join([k.acc_64[layer, 3], vectors]),
         )
         rows = k.share.shape[2]
         for at, block in enumerate(blocks):
@@ -413,77 +421,146 @@
                     piece * rows : (piece + 1) * rows, :
                 ]
 
-        finish_exchange(copy)
+    def own_rows(layer):
+        summed = k.scatter[...]
+        coarse = summed.astype(BF16)
+        fine = (summed - coarse.astype(F32)).astype(BF16)
+        back = k.small[layer, SENDER_B]
+        first_sum = k.first_sum[...].astype(BF16)
+        for part in range(locals_):
+            span = slice(part * wide, (part + 1) * wide)
+            place = slice(part * high, (part + 1) * high)
+            into(layer)[:, place] += (
+                dot(back, coarse[span])
+                + dot(back, fine[span])
+                + dot(k.small[layer, RECEIVER_B], first_sum[:, place])
+            )
+
+    def take_back(layer):
+        finish_exchange(exchange(k.gives, k.backs, k.back_send, k.back_recv, layer))
         returned = join([k.backs[layer, way] for way in range(4)])
-        into[:, :LISTED] += dot_nt(returned, k.owner[...])
-
-    def reduce_layer(layer):
-        def band_copy(source, landing, sends, recvs, piece, slot, other):
-            return pltpu.make_async_remote_copy(
-                src_ref=source.at[layer, piece],
-                dst_ref=landing.at[layer, slot],
-                send_sem=sends.at[layer, other],
-                recv_sem=recvs.at[layer, slot],
-                device_id=(other, lon),
-                device_id_type=MESH,
-            )
-
-        def scatter_start(step, carry):
-            other = lax.rem(band + step, bands)
-            band_copy(k.share, k.spread, k.rs_send, k.rs_recv, other, band, other).start()
+        into(layer)[:, :LISTED] += dot_nt(returned, k.owner[...])
+
+    def band_copy(layer, source, landing, sends, recvs, piece, slot, other):
+        return pltpu.make_async_remote_copy(
+            src_ref=source.at[layer, piece],
+            dst_ref=landing.at[layer, slot],
+            send_sem=sends.at[layer, other],
+            recv_sem=recvs.at[layer, slot],
+            device_id=(other, lon),
+            device_id_type=MESH,
+        )
+
+    def lon_copy(layer, slot, other):
+        return pltpu.make_async_remote_copy(
+            src_ref=k.swap.at[layer, lon],
+            dst_ref=k.swap.at[layer, slot],
+            send_sem=k.sw_send.at[layer, other],
+            recv_sem=k.sw_recv.at[layer, slot],
+            device_id=(band, other),
+            device_id_type=MESH,
+        )
+
+    def over(count_, here, act):
+        def step(at, carry):
+            act(lax.rem(here + at, count_))
             return carry
 
-        def scatter_end(step, carry):
-            other = lax.rem(band + step, bands)
-            band_copy(k.share, k.spread, k.rs_send, k.rs_recv, other, other, other).wait()
-            return carry
-
-        lax.fori_loop(1, bands, scatter_start, 0)
+        lax.fori_loop(1, count_, step, 0)
+
+    def spread_start(layer):
+        over(
+            bands,
+            band,
+            lambda other: band_copy(
+                layer, k.share, k.spread, k.rs_send, k.rs_recv, other, band, other
+            ).start(),
+        )
         k.spread[layer, band] = k.share[layer, band]
-        lax.fori_loop(1, bands, scatter_end, 0)
+
+    def swap_start(layer):
+        over(
+            bands,
+            band,
+            lambda other: band_copy(
+                layer, k.share, k.spread, k.rs_send, k.rs_recv, other, other, other
+            ).wait(),
+        )
         k.swap[layer, lon] = jnp.sum(k.spread[layer], axis=0)
-
-        def lon_copy(slot, other):
-            return pltpu.make_async_remote_copy(
-                src_ref=k.swap.at[layer, lon],
-                dst_ref=k.swap.at[layer, slot],
-                send_sem=k.sw_send.at[layer, other],
-                recv_sem=k.sw_recv.at[layer, slot],
-                device_id=(band, other),
-                device_id_type=MESH,
-            )
-
-        def swap_start(step, carry):
-            lon_copy(lon, lax.rem(lon + step, lons)).start()
-            return carry
-
-        def swap_end(step, carry):
-            other = lax.rem(lon + step, lons)
-            lon_copy(other, other).wait()
-            return carry
-
-        lax.fori_loop(1, lons, swap_start, 0)
-        lax.fori_loop(1, lons, swap_end, 0)
+        over(lons, lon, lambda other: lon_copy(layer, lon, other).start())
+
+    def gather_start(layer):
+        over(lons, lon, lambda other: lon_copy(layer, other, other).wait())
         k.whole[layer, band] = jnp.sum(k.swap[layer], axis=0)
-
-        def gather_start(step, carry):
-            other = lax.rem(band + step, bands)
-            band_copy(k.whole, k.whole, k.ag_send, k.ag_recv, band, band, other).start()
-            return carry
-
-        def gather_end(step, carry):
-            other = lax.rem(band + step, bands)
-            band_copy(k.whole, k.whole, k.ag_send, k.ag_recv, band, other, other).wait()
-            return carry
-
-        lax.fori_loop(1, bands, gather_start, 0)
-        lax.fori_loop(1, bands, gather_end, 0)
-
-        rows = k.share.shape[2]
+        over(
+            bands,
+            band,
+            lambda other: band_copy(
+                layer, k.whole, k.whole, k.ag_send, k.ag_recv, band, band, other
+            ).start(),
+        )
+
+    def gather_end(layer):
+        over(
+            bands,
+            band,
+            lambda other: band_copy(
+                layer, k.whole, k.whole, k.ag_send, k.ag_recv, band, other, other
+            ).wait(),
+        )
+        for piece in range(k.reduced.shape[1]):
+            k.reduced[layer, piece] = k.whole[layer, piece]
+
+    middle_row = nodes // 2
+    k.xs[0, :wide, :] = k.state[...]
+    k.sums[...] = jnp.zeros_like(k.sums)
+    k.acc_64[...] = jnp.zeros_like(k.acc_64)
+    k.acc_128[...] = jnp.zeros_like(k.acc_128)
+    pl.semaphore_wait(barrier, bands + lons - 2)
+    send_halos(0)
+    project(0)
+    project_halos(0)
+    edges_forward(0)
+    nodes_forward(0, 0, LISTED)
+    send_halos(1)
+    nodes_forward(0, LISTED, nodes)
+    project(1)
+    project_halos(1)
+    edges_forward(1)
+    nodes_forward(1, 0, nodes)
+    nodes_backward(1, 0, nodes)
+    edges_backward(1)
+    give_back(1)
+    spread_start(1)
+    own_rows(1)
+    nodes_backward(0, LISTED, nodes)
+    take_back(1)
+    nodes_backward(0, 0, LISTED)
+    swap_start(1)
+    edges_backward(0)
+    give_back(0)
+    spread_start(0)
+    gather_start(1)
+    own_rows(0)
+    take_back(0)
+    swap_start(0)
+    gather_start(0)
+    gather_end(1)
+    gather_end(0)
+
+
+def finish(names, *refs):
+    k = types.SimpleNamespace(**dict(zip(names, refs)))
+    wide = k.g_ew2.shape[1]
+    k.mesh_out[...] = k.mesh_in[...]
+    k.grad_state[...] = k.state_in[...]
+    k.grad_latent[...] = k.latent_in[...]
+    for layer in range(2):
+        rows = k.reduced.shape[2]
         pieces = wide // rows
         blocks = []
         for at in range(4):
-            block = [k.whole[layer, at * pieces + piece] for piece in range(pieces)]
+            block = [k.reduced[layer, at * pieces + piece] for piece in range(pieces)]
             blocks.append(block[0] if pieces == 1 else jnp.concatenate(block, axis=0))
         k.g_ew1t[layer, :, : 2 * wide] = blocks[0]
         k.g_ew1t[layer, :, 2 * wide :] = blocks[1][:, :wide]
@@ -496,14 +573,6 @@
         ):
             out[layer : layer + 1, :] = lines[which : which + 1, :]
 
-    k.xs[0, :wide, :] = k.state[...]
-    forward(0)
-    forward(1)
-    backward(1)
-    backward(0)
-    reduce_layer(1)
-    reduce_layer(0)
-
 
 INPUTS = (
     "state", "latent", "attr", "nbr", "lists", "count", "cmask", "ew1t", "eb1", "ew2",
@@ -513,6 +582,11 @@
     "mesh_out", "grad_state", "grad_latent", "g_ew1t", "g_eb1", "g_ew2", "g_egain",
     "g_eshift", "g_nw1t", "g_nb1", "g_nw2", "g_ngain", "g_nshift",
 )
+
+
+FIRST_OUTPUTS = ("mesh_out", "grad_state", "grad_latent", "reduced")
+FINISH_INPUTS = ("mesh_in", "state_in", "latent_in", "reduced")
+VMEM_BYTES = 60 * 2**20
 
 
 def shards(bands, lons, *args):
@@ -576,10 +650,13 @@
         rate_n=pltpu.VMEM((2, 1, nodes), F32),
         unit_n=pltpu.VMEM((2, wide, nodes), F32),
         middle=pltpu.VMEM((wide, nodes), F32),
+        scaled=pltpu.VMEM((wide, nodes), F32),
+        center=pltpu.VMEM((wide, nodes), F32),
+        first_sum=pltpu.VMEM((wide, nodes), F32),
         scatter=pltpu.VMEM((parts * wide, high), F32),
-        sums=pltpu.VMEM((6, wide, 128), F32),
-        acc_64=pltpu.VMEM((4, wide, wide), F32),
-        acc_128=pltpu.VMEM((wide, 2 * wide), F32),
+        sums=pltpu.VMEM((2, 6, wide, 128), F32),
+        acc_64=pltpu.VMEM((2, 4, wide, wide), F32),
+        acc_128=pltpu.VMEM((2, wide, 2 * wide), F32),
         halo_send=sem((2, 4)),
         halo_recv=sem((2, 4)),
         back_send=sem((2, 4)),
@@ -594,15 +671,15 @@
     vmem = pl.BlockSpec(memory_space=pltpu.VMEM)
     specs = [vmem] * len(INPUTS)
     specs[INPUTS.index("count")] = pl.BlockSpec(memory_space=pltpu.SMEM)
-    names = INPUTS + OUTPUTS + tuple(scratch)
-    result = pl.pallas_call(
-        functools.partial(kernel, names, bands, lons),
-        out_shape=outs,
+    first_outs = outs[:3] + (shape((2, pieces, rows, 128), F32),)
+    mids = pl.pallas_call(
+        functools.partial(kernel, INPUTS + FIRST_OUTPUTS + tuple(scratch), bands, lons),
+        out_shape=first_outs,
         in_specs=specs,
-        out_specs=(vmem,) * len(OUTPUTS),
+        out_specs=(vmem,) * 4,
         scratch_shapes=list(scratch.values()),
         compiler_params=pltpu.CompilerParams(
-            collective_id=0, has_side_effects=True, vmem_limit_bytes=60 * 2**20
+            collective_id=0, has_side_effects=True, vmem_limit_bytes=VMEM_BYTES
         ),
         name="layers",
     )(
@@ -625,6 +702,13 @@
         node_shift,
         out_grad.T,
     )
+    result = pl.pallas_call(
+        functools.partial(finish, FINISH_INPUTS + OUTPUTS),
+        out_shape=outs,
+        in_specs=(vmem,) * 4,
+        out_specs=(vmem,) * 13,
+        name="finish",
+    )(*mids)
     result = list(result)
     for at in range(3):
         result[at] = result[at].T

time: 125 us -> 86.7 us (0.69)
  local copies, waits for them, and re-layouts: 18.8 us -> 0 us
  Pallas kernels: 104 us -> 85.2 us
    pallas_call x1 -> x2, Pallas kernels: 104 us -> 85.2 us  [the longest x1 82.5 us: shards(): pl.pallas_call(functools.partial(kernel, INPUTS + FIRST_OUTPUTS + tuple(s...]
    unnamed x13 -> x0, local copies, waits for them, and re-layouts: 18.8 us -> none
where the time goes in v2:
time: 86.7 us; the launch traced here: 86.5 us
  Pallas kernels  85.2 us (98%)
  between operations  1.31 us (2%)
    pallas_call x1, Pallas kernels, shards(): pl.pallas_call(functools.partial(kernel, INPUTS + FIRST_OUTPUTS + tuple(s...  82.5 us
    pallas_call x1, Pallas kernels, shards(): pl.pallas_call(functools.partial(finish, FINISH_INPUTS + OUTPUTS), out_sh...  2.74 us

profile of v2, /device:TPU:0, one launch (start us, length us, event | category | flops | bytes accessed | tf_op | source)
XLA Modules:
  0.0 86.5 jit_solution(38513138076673860)
XLA Ops:
  1.3 82.5 %layers.1 = (bf16[64,2048]{1,0:T(8,128)(2,1)}, f32[64,2048]{1,0:T(8,128)}, f32[64,2048]{1,0:T(8,128)}, f32[2,8,32,128]{3,2,1,0:T(8,128)}) custom-call(bf16[64,2048]{1,0:T(8,128)(2,1)} %bitcast.13, bf16[64,2048]{1,0:T(8,128)(2,1)} %bitcast.14, bf16[2,8,64,2048]{3,2,1,0:T(8,128)(2,1)} %bitcast.12, s32[2,8,2048]{2,1,0:T(8,128)} %bitcast.16, s32[4,128]{1,0:T(4,128)} %refs_4_.1, ...), custom_call_target="tpu_custom_call" | custom-call | tf_op jit(solution)/shard_map/layers/pallas_call | solution.py:675
  83.8 2.7 %finish.1 = (bf16[64,2048]{1,0:T(8,128)(2,1)}, f32[64,2048]{1,0:T(8,128)}, f32[64,2048]{1,0:T(8,128)}, f32[2,64,192]{2,1,0:T(8,128)}, f32[2,64]{1,0:T(2,128)}, /...) custom-call(bf16[64,2048]{1,0:T(8,128)(2,1)} %get-tuple-element.30.r, ...), custom_call_target="tpu_custom_call" | custom-call | tf_op jit(solution)/shard_map/finish/pallas_call | solution.py:705

commit v3 on v2

--- a/solution.py
+++ b/solution.py
@@ -12,8 +12,9 @@
 BF16 = jnp.bfloat16
 MESH = pl.DeviceIdType.MESH
 LISTED = 1024
-TILE = 256
-GROUP = 4
+TILE_F, TILE_B, TILE_S = 2048, 1024, 1024
+GROUP_F, GROUP_B, GROUP_S = 1, 2, 2
+WAYS = 4
 CHUNK = 256
 EB1, EGAIN, ESHIFT, NB1, NGAIN, NSHIFT, CMASK = range(7)
 
@@ -77,11 +78,35 @@
     wide, nodes = k.state.shape
     degree = k.nbr.shape[1]
     halo = k.lists.shape[1]
-    high = 4 * halo
+    high = WAYS * halo
     shift = high.bit_length() - 1
     locals_ = nodes // high
-    parts = locals_ + 1
+    parts = locals_ + 4 // WAYS
     count = k.count[0]
+    loads = [
+        pltpu.make_async_copy(source, target, k.load_sem.at[at])
+        for at, (source, target) in enumerate(
+            (
+                (k.attr_in.at[0], k.attr.at[0]),
+                (k.attr_in.at[1], k.attr.at[1]),
+                (k.latent_in, k.latent),
+                (k.out_grad_in, k.out_grad),
+            )
+        )
+    ]
+    stores = [
+        pltpu.make_async_copy(source, target, k.store_sem.at[at])
+        for at, (source, target) in enumerate(
+            (
+                (k.mesh_out, k.mesh_to),
+                (k.grad_latent, k.latent_to),
+                (k.grad_state, k.state_to),
+                (k.whole, k.reduced),
+            )
+        )
+    ]
+    for load in loads:
+        load.start()
     west, east = lax.rem(lon + lons - 1, lons), lax.rem(lon + 1, lons)
     has_low, has_high = band > 0, band < bands - 1
 
@@ -146,52 +171,55 @@
             else:
                 end()
 
-    for at, rows in enumerate((k.eb1, k.egain, k.eshift, k.nb1, k.ngain, k.nshift)):
-        k.vrows[2 * at : 2 * at + 2, :] = rows[...]
-    k.vrows[12:14, :] = k.cmask[...].astype(F32)
-    k.vrows[14:16, :] = jnp.zeros((2, wide), F32)
-    k.cols[...] = exact_dot(eye(wide, F32), k.vrows[...], ((1,), (1,)))
+    SENDER, RECEIVER, ATTR, SECOND, NODE_TWO, SENDER_B, RECEIVER_B, SECOND_B, NODE_TWO_B = range(9)
 
     def col(layer, which):
         at = 2 * which + layer
         return k.cols[:, at : at + 1]
 
-    for way in range(4):
-        k.owner[:, way * halo : (way + 1) * halo] = one_hot(k.lists[way : way + 1, :], LISTED)
-
-    weights = []
-    for layer in range(2):
-        w1t = k.ew1t[layer]
-        n1t = k.nw1t[layer]
-        w2 = k.ew2[layer]
-        n2 = k.nw2[layer]
-        half = BF16(0.5)
-        weights.append(
-            dict(
-                sender=w1t[:, :wide] * half,
-                receiver=w1t[:, wide : 2 * wide] * half,
-                attr=w1t[:, 2 * wide :] * half,
-                second=turned(w2),
-                node_one=n1t * half,
-                node_two=turned(n2),
-                sender_back=turned(w1t[:, :wide]),
-                receiver_back=turned(w1t[:, wide : 2 * wide]),
-                second_back=w2 * half,
-                node_one_back=turned(n1t),
-                node_two_back=n2 * half,
+    def tables():
+        for at, rows in enumerate((k.eb1, k.egain, k.eshift, k.nb1, k.ngain, k.nshift)):
+            k.vrows[2 * at : 2 * at + 2, :] = rows[...]
+        k.vrows[12:14, :] = k.cmask[...].astype(F32)
+        k.vrows[14:16, :] = jnp.zeros((2, wide), F32)
+        k.cols[...] = exact_dot(eye(wide, F32), k.vrows[...], ((1,), (1,)))
+
+        weights = []
+        for layer in range(2):
+            w1t = k.ew1t[layer]
+            n1t = k.nw1t[layer]
+            w2 = k.ew2[layer]
+            n2 = k.nw2[layer]
+            half = BF16(0.5)
+            weights.append(
+                dict(
+                    sender=w1t[:, :wide] * half,
+                    receiver=w1t[:, wide : 2 * wide] * half,
+                    attr=w1t[:, 2 * wide :] * half,
+                    second=turned(w2),
+                    node_one=n1t * half,
+                    node_two=turned(n2),
+                    sender_back=turned(w1t[:, :wide]),
+                    receiver_back=turned(w1t[:, wide : 2 * wide]),
+                    second_back=w2 * half,
+                    node_one_back=turned(n1t),
+                    node_two_back=n2 * half,
+                )
             )
-        )
-    for layer in range(2):
-        for at, name in enumerate(
-            (
-                "sender", "receiver", "attr", "second", "node_two",
-                "sender_back", "receiver_back", "second_back", "node_two_back",
-            )
-        ):
-            k.small[layer, at] = weights[layer][name]
-        k.wide_w[layer] = weights[layer]["node_one"]
-        k.tall_w[layer] = weights[layer]["node_one_back"]
-    SENDER, RECEIVER, ATTR, SECOND, NODE_TWO, SENDER_B, RECEIVER_B, SECOND_B, NODE_TWO_B = range(9)
+        for layer in range(2):
+            for at, name in enumerate(
+                (
+                    "sender", "receiver", "attr", "second", "node_two",
+                    "sender_back", "receiver_back", "second_back", "node_two_back",
+                )
+            ):
+                k.small[layer, at] = weights[layer][name]
+            k.wide_w[layer] = weights[layer]["node_one"]
+            k.tall_w[layer] = weights[layer]["node_one_back"]
+
+    def owners():
+        for way in range(4):
+            k.owner[:, way * halo : (way + 1) * halo] = one_hot(k.lists[way : way + 1, :], LISTED)
 
     def split_index(layer, lanes):
         index = k.nbr[layer, :, lanes]
@@ -209,26 +237,29 @@
             k.sends[layer, way] = picked[:, way * halo : (way + 1) * halo]
         start_exchange(exchange(k.sends, k.halos, k.halo_send, k.halo_recv, layer))
 
+    def as_sent(layer, rows):
+        return rows if layer == 0 else dot(k.small[layer, SENDER], rows).astype(BF16)
+
     def project(layer):
         low = k.xs[layer, :wide, :]
-        k.base[...] = dot(k.small[layer, RECEIVER], low) + 0.5 * col(layer, EB1)
-        projected = dot(k.small[layer, SENDER], low).astype(BF16)
+        own = as_sent(layer, low)
         for part in range(locals_):
-            k.table[part * wide : (part + 1) * wide, :] = projected[
-                :, part * high : (part + 1) * high
-            ]
+            k.table[part * wide : (part + 1) * wide, :] = own[:, part * high : (part + 1) * high]
+        base = dot(k.small[layer, RECEIVER], low) + 0.5 * col(layer, EB1)
+        loads[layer].wait()
+        for j in range(degree):
+            k.pre[j] = dot(k.small[layer, ATTR], k.attr[layer, j]) + base
 
     def project_halos(layer):
         finish_exchange(exchange(k.sends, k.halos, k.halo_send, k.halo_recv, layer))
         for way in range(4):
-            k.table[locals_ * wide :, way * halo : (way + 1) * halo] = dot(
-                k.small[layer, SENDER], k.halos[layer, way]
-            ).astype(BF16)
+            top, left = (locals_ + way // WAYS) * wide, way % WAYS * halo
+            k.table[top : top + wide, left : left + halo] = as_sent(layer, k.halos[layer, way])
 
     def edges_forward(layer):
         def body(at, carry):
-            start = pl.multiple_of(at * TILE, TILE)
-            lanes = pl.ds(start, TILE)
+            start = pl.multiple_of(at * TILE_F, TILE_F)
+            lanes = pl.ds(start, TILE_F)
             index, sub, hi = split_index(layer, lanes)
             sender_ok = jnp.where(
                 index < nodes,
@@ -239,22 +270,25 @@
                     jnp.where(index < nodes + 2 * halo, has_high.astype(F32), 1.0),
                 ),
             )
-            edge_ok = sender_ok * live_lanes(start, TILE).astype(F32)
-            base = k.base[:, lanes]
-            total = jnp.zeros((wide, TILE), F32)
-            for first in range(0, degree, GROUP):
-                slots = range(first, first + GROUP)
+            edge_ok = sender_ok * live_lanes(start, TILE_F).astype(F32)
+            total = jnp.zeros((wide, TILE_F), F32)
+            for first in range(0, degree, GROUP_F):
+                slots = range(first, first + GROUP_F)
                 hot = join([one_hot(hi[j : j + 1], high) for j in slots])
                 found = dot(k.table[...], hot)
                 for place, j in enumerate(slots):
-                    piece = found[:, place * TILE : (place + 1) * TILE]
-                    piece = piece.reshape(parts, wide // 8, 8, TILE)
-                    which = jnp.broadcast_to(sub[j : j + 1], (8, TILE))
+                    piece = found[:, place * TILE_F : (place + 1) * TILE_F]
+                    piece = piece.reshape(parts, wide // 8, 8, TILE_F)
+                    which = jnp.broadcast_to(sub[j : j + 1], (8, TILE_F))
                     chosen = piece[0]
                     for part in range(1, parts):
                         chosen = jnp.where((which == part)[None], piece[part], chosen)
-                    own = dot(k.small[layer, ATTR], k.attr[layer, j, :, lanes])
-                    act, slope = gate(chosen.reshape(wide, TILE) + base + own)
+                    chosen = chosen.reshape(wide, TILE_F)
+                    if layer == 0:
+                        chosen = chosen.astype(BF16)
+                        k.senders[j, :, lanes] = chosen
+                        chosen = dot(k.small[layer, SENDER], chosen)
+                    act, slope = gate(chosen + k.pre[j, :, lanes])
                     act = act.astype(BF16)
                     k.act[layer, j, :, lanes] = act
                     k.slope[layer, j, :, lanes] = slope.astype(BF16)
@@ -269,7 +303,7 @@
             k.kept[layer, :, lanes] = jnp.sum(edge_ok, axis=0, keepdims=True)
             return carry
 
-        lax.fori_loop(0, nodes // TILE, body, 0)
+        lax.fori_loop(0, nodes // TILE_F, body, 0)
 
     def nodes_forward(layer, first, last):
         for lanes in node_lanes(first, last):
@@ -331,19 +365,44 @@
             k.scaled[:, lanes] = scaled
             k.center[:, lanes] = scaled - mean0(scaled)
 
+    def scatter_slots(lanes, sub, hi, firsts, slots):
+        spreads, hots = [], []
+        for j, grad in zip(slots, firsts):
+            width = grad.shape[1]
+            which = jnp.broadcast_to(sub[j : j + 1].astype(jnp.int16), (16, width))
+            rows = grad.reshape(wide // 16, 16, width)
+            spreads.append(
+                jnp.concatenate(
+                    [
+                        jnp.where((which == part)[None], rows, BF16(0)).reshape(wide, width)
+                        for part in range(parts)
+                    ],
+                    axis=0,
+                )
+            )
+            hots.append(one_hot(hi[j : j + 1], high))
+        k.scatter[...] += dot_nt(join(spreads), join(hots))
+
+    def scatter_pass(layer, first, last):
+        def body(at, carry):
+            lanes = pl.ds(pl.multiple_of(at * TILE_S, TILE_S), TILE_S)
+            index, sub, hi = split_index(layer, lanes)
+            for start in range(0, degree, GROUP_S):
+                slots = range(start, start + GROUP_S)
+                scatter_slots(lanes, sub, hi, [k.first[j, :, lanes] for j in slots], slots)
+            return carry
+
+        lax.fori_loop(first, last, body, 0)
+
     def edges_backward(layer):
-        k.scatter[...] = jnp.zeros_like(k.scatter)
-
         def body(at, carry):
-            lanes = pl.ds(pl.multiple_of(at * TILE, TILE), TILE)
+            lanes = pl.ds(pl.multiple_of(at * TILE_B, TILE_B), TILE_B)
             index, sub, hi = split_index(layer, lanes)
             scaled, center = k.scaled[:, lanes], k.center[:, lanes]
-            first_sum = jnp.zeros((wide, TILE), F32)
-            grad_two = jnp.zeros((wide, wide), F32)
-            grad_attr = jnp.zeros((wide, wide), F32)
-            for first in range(0, degree, GROUP):
-                slots = range(first, first + GROUP)
-                hots, spreads, seconds, firsts = [], [], [], []
+            first_sum = jnp.zeros((wide, TILE_B), F32)
+            for start in range(0, degree, GROUP_B):
+                slots = range(start, start + GROUP_B)
+                firsts = []
                 for j in slots:
                     unit = k.unit[layer, j, :, lanes].astype(F32)
                     second = (center - unit * mean0(scaled * unit)) * k.rate_e[
@@ -355,53 +414,67 @@
                     ].astype(F32)
                     first_sum = first_sum + grad_one
                     grad_one = grad_one.astype(BF16)
-                    which = jnp.broadcast_to(sub[j : j + 1].astype(jnp.int16), (16, TILE))
-                    rows = grad_one.reshape(wide // 16, 16, TILE)
-                    spreads.append(
-                        jnp.concatenate(
-                            [
-                                jnp.where((which == part)[None], rows, BF16(0)).reshape(wide, TILE)
-                                for part in range(parts)
-                            ],
-                            axis=0,
-                        )
-                    )
-                    hots.append(one_hot(hi[j : j + 1], high))
-                    seconds.append(second)
+                    k.first[j, :, lanes] = grad_one
+                    k.second[j, :, lanes] = second
                     firsts.append(grad_one)
-                k.scatter[...] += dot_nt(join(spreads), join(hots))
-                grad_two = grad_two + dot_nt(
-                    join([k.act[layer, j, :, lanes] for j in slots]), join(seconds)
-                )
-                grad_attr = grad_attr + dot_nt(
-                    join(firsts), join([k.attr[layer, j, :, lanes] for j in slots])
-                )
+                if layer == 1:
+                    scatter_slots(lanes, sub, hi, firsts, slots)
             k.first_sum[:, lanes] = first_sum
-            k.acc_64[layer, 1] += grad_attr
-            k.acc_64[layer, 2] += grad_two
             return carry
 
-        lax.fori_loop(0, nodes // TILE, body, 0)
+        lax.fori_loop(0, nodes // TILE_B, body, 0)
+
+    def edge_weights(layer):
+        grad_two = jnp.zeros((wide, wide), F32)
+        grad_attr = jnp.zeros((wide, wide), F32)
+        grad_both = jnp.zeros((wide, 2 * wide), F32)
+        for j in range(degree):
+            grad_two = grad_two + dot_nt(k.act[layer, j], k.second[j])
+            if layer == 0:
+                both = jnp.concatenate([k.senders[j], k.attr[layer, j]], axis=0)
+                grad_both = grad_both + dot_nt(k.first[j], both)
+            else:
+                grad_attr = grad_attr + dot_nt(k.first[j], k.attr[layer, j])
+        k.acc_64[layer, 2] = grad_two
+        if layer == 0:
+            k.acc_64[layer, 0] = grad_both[:, :wide]
+            k.acc_64[layer, 1] = grad_both[:, wide:]
+        else:
+            k.acc_64[layer, 1] = grad_attr
+
+    def two_terms(values):
+        coarse = values.astype(BF16)
+        return coarse, (values - coarse.astype(F32)).astype(BF16)
 
     def give_back(layer):
-        summed = k.scatter[...]
-        coarse = summed.astype(BF16)
-        fine = (summed - coarse.astype(F32)).astype(BF16)
         back = k.small[layer, SENDER_B]
-        last = slice(locals_ * wide, parts * wide)
-        to_owner = (dot(back, coarse[last]) + dot(back, fine[last])).astype(BF16)
+        halo_sums = [
+            two_terms(k.scatter[part * wide : (part + 1) * wide, :])
+            for part in range(locals_, parts)
+        ]
+        to_owner = join([dot(back, coarse) + dot(back, fine) for coarse, fine in halo_sums])
+        to_owner = to_owner.astype(BF16)
         for way in range(4):
             k.gives[layer, way] = to_owner[:, way * halo : (way + 1) * halo]
         start_exchange(exchange(k.gives, k.backs, k.back_send, k.back_recv, layer))
+
+    def sender_weights(layer):
+        sender = jnp.zeros((wide, wide), F32)
+        for part in range(parts):
+            if part < locals_:
+                rows = k.xs[layer, :wide, part * high : (part + 1) * high]
+            else:
+                first = (part - locals_) * WAYS
+                rows = join([k.halos[layer, first + way] for way in range(WAYS)])
+            coarse, fine = two_terms(k.scatter[part * wide : (part + 1) * wide, :])
+            sender = sender + dot_nt(coarse, rows) + dot_nt(fine, rows)
+        k.acc_64[layer, 0] = sender
+
+    def share_weights(layer):
         k.sums[layer, EB1] = fold(k.first_sum[...])
         first_sum = k.first_sum[...].astype(BF16)
         receiver = dot_nt(first_sum, k.xs[layer, :wide, :])
-        halo_rows = join([k.halos[layer, way] for way in range(4)])
-        sender = dot_nt(coarse[last], halo_rows) + dot_nt(fine[last], halo_rows)
-        for part in range(locals_):
-            span = slice(part * wide, (part + 1) * wide)
-            rows = k.xs[layer, :wide, part * high : (part + 1) * high]
-            sender = sender + dot_nt(coarse[span], rows) + dot_nt(fine[span], rows)
+        sender = k.acc_64[layer, 0]
         lane = lax.broadcasted_iota(jnp.int32, (wide, wide), 1)
         vectors = jnp.zeros((wide, wide), F32)
         for which in range(6):
@@ -422,17 +495,14 @@
                 ]
 
     def own_rows(layer):
-        summed = k.scatter[...]
-        coarse = summed.astype(BF16)
-        fine = (summed - coarse.astype(F32)).astype(BF16)
         back = k.small[layer, SENDER_B]
         first_sum = k.first_sum[...].astype(BF16)
         for part in range(locals_):
-            span = slice(part * wide, (part + 1) * wide)
             place = slice(part * high, (part + 1) * high)
+            coarse, fine = two_terms(k.scatter[part * wide : (part + 1) * wide, :])
             into(layer)[:, place] += (
-                dot(back, coarse[span])
-                + dot(back, fine[span])
+                dot(back, coarse)
+                + dot(back, fine)
                 + dot(k.small[layer, RECEIVER_B], first_sum[:, place])
             )
 
@@ -508,45 +578,62 @@
                 layer, k.whole, k.whole, k.ag_send, k.ag_recv, band, other, other
             ).wait(),
         )
-        for piece in range(k.reduced.shape[1]):
-            k.reduced[layer, piece] = k.whole[layer, piece]
-
-    middle_row = nodes // 2
+
     k.xs[0, :wide, :] = k.state[...]
+    owners()
+    pl.semaphore_wait(barrier, bands + lons - 2)
+    send_halos(0)
+    tables()
     k.sums[...] = jnp.zeros_like(k.sums)
     k.acc_64[...] = jnp.zeros_like(k.acc_64)
     k.acc_128[...] = jnp.zeros_like(k.acc_128)
-    pl.semaphore_wait(barrier, bands + lons - 2)
-    send_halos(0)
+    k.scatter[...] = jnp.zeros_like(k.scatter)
     project(0)
     project_halos(0)
     edges_forward(0)
+    loads[2].wait()
     nodes_forward(0, 0, LISTED)
     send_halos(1)
     nodes_forward(0, LISTED, nodes)
     project(1)
     project_halos(1)
     edges_forward(1)
+    loads[3].wait()
     nodes_forward(1, 0, nodes)
+    stores[0].start()
     nodes_backward(1, 0, nodes)
     edges_backward(1)
     give_back(1)
+    edge_weights(1)
+    sender_weights(1)
+    share_weights(1)
     spread_start(1)
     own_rows(1)
     nodes_backward(0, LISTED, nodes)
     take_back(1)
+    stores[1].start()
     nodes_backward(0, 0, LISTED)
     swap_start(1)
     edges_backward(0)
-    give_back(0)
+    edge_weights(0)
+    share_weights(0)
     spread_start(0)
     gather_start(1)
+    k.scatter[...] = jnp.zeros_like(k.scatter)
+    steps = nodes // TILE_S
+    scatter_pass(0, 0, steps // 2)
+    swap_start(0)
+    scatter_pass(0, steps // 2, steps)
+    give_back(0)
+    gather_start(0)
     own_rows(0)
     take_back(0)
-    swap_start(0)
-    gather_start(0)
+    stores[2].start()
     gather_end(1)
     gather_end(0)
+    stores[3].start()
+    for store in stores:
+        store.wait()
 
 
 def finish(names, *refs):
@@ -575,8 +662,8 @@
 
 
 INPUTS = (
-    "state", "latent", "attr", "nbr", "lists", "count", "cmask", "ew1t", "eb1", "ew2",
-    "egain", "eshift", "nw1t", "nb1", "nw2", "ngain", "nshift", "out_grad",
+    "state", "latent_in", "attr_in", "nbr", "lists", "count", "cmask", "ew1t", "eb1", "ew2",
+    "egain", "eshift", "nw1t", "nb1", "nw2", "ngain", "nshift", "out_grad_in",
 )
 OUTPUTS = (
     "mesh_out", "grad_state", "grad_latent", "g_ew1t", "g_eb1", "g_ew2", "g_egain",
@@ -584,7 +671,7 @@
 )
 
 
-FIRST_OUTPUTS = ("mesh_out", "grad_state", "grad_latent", "reduced")
+FIRST_OUTPUTS = ("mesh_to", "state_to", "latent_to", "reduced")
 FINISH_INPUTS = ("mesh_in", "state_in", "latent_in", "reduced")
 VMEM_BYTES = 60 * 2**20
 
@@ -598,8 +685,8 @@
     nodes, wide = node_state.shape
     degree = neighbours.shape[2]
     halo = halo_lists.shape[1]
-    high = 4 * halo
-    parts = nodes // high + 1
+    high = WAYS * halo
+    parts = nodes // high + 4 // WAYS
     rows = max(8, 4 * wide // bands)
     while wide % rows:
         rows //= 2
@@ -632,12 +719,23 @@
         whole=pltpu.VMEM((2, pieces, rows, 128), F32),
         vrows=pltpu.VMEM((16, wide), F32),
         cols=pltpu.VMEM((wide, 16), F32),
-        owner=pltpu.VMEM((LISTED, high), BF16),
+        owner=pltpu.VMEM((LISTED, 4 * halo), BF16),
         small=pltpu.VMEM((2, 9, wide, wide), BF16),
         wide_w=pltpu.VMEM((2, wide, 2 * wide), BF16),
         tall_w=pltpu.VMEM((2, 2 * wide, wide), BF16),
         xs=pltpu.VMEM((2, 2 * wide, nodes), BF16),
-        base=pltpu.VMEM((wide, nodes), F32),
+        attr=pltpu.VMEM((2, degree, wide, nodes), BF16),
+        latent=pltpu.VMEM((wide, nodes), BF16),
+        out_grad=pltpu.VMEM((wide, nodes), BF16),
+        mesh_out=pltpu.VMEM((wide, nodes), BF16),
+        grad_latent=pltpu.VMEM((wide, nodes), F32),
+        grad_state=pltpu.VMEM((wide, nodes), F32),
+        load_sem=sem((4,)),
+        store_sem=sem((4,)),
+        pre=pltpu.VMEM((degree, wide, nodes), F32),
+        senders=pltpu.VMEM((degree, wide, nodes), BF16),
+        first=pltpu.VMEM((degree, wide, nodes), BF16),
+        second=pltpu.VMEM((degree, wide, nodes), BF16),
         table=pltpu.VMEM((parts * wide, high), BF16),
         act=pltpu.VMEM((2, degree, wide, nodes), BF16),
         slope=pltpu.VMEM((2, degree, wide, nodes), BF16),
@@ -670,13 +768,16 @@
     )
     vmem = pl.BlockSpec(memory_space=pltpu.VMEM)
     specs = [vmem] * len(INPUTS)
+    anywhere = pl.BlockSpec(memory_space=pl.ANY)
     specs[INPUTS.index("count")] = pl.BlockSpec(memory_space=pltpu.SMEM)
+    for name in ("latent_in", "attr_in", "out_grad_in"):
+        specs[INPUTS.index(name)] = anywhere
     first_outs = outs[:3] + (shape((2, pieces, rows, 128), F32),)
     mids = pl.pallas_call(
         functools.partial(kernel, INPUTS + FIRST_OUTPUTS + tuple(scratch), bands, lons),
         out_shape=first_outs,
         in_specs=specs,
-        out_specs=(vmem,) * 4,
+        out_specs=(anywhere,) * 4,
         scratch_shapes=list(scratch.values()),
         compiler_params=pltpu.CompilerParams(
             collective_id=0, has_side_effects=True, vmem_limit_bytes=VMEM_BYTES

time: 86.7 us -> 76 us (0.88)
  Pallas kernels: 85.2 us -> 74.4 us
    pallas_call x1, Pallas kernels: 82.5 us -> 71.6 us  [shards(): pl.pallas_call(functools.partial(kernel, INPUTS + FIRST_OUTPUTS + tuple(s...]
where the time goes in v3:
time: 76 us; the launch traced here: 75.8 us
  Pallas kernels  74.4 us (98%)
  between operations  1.44 us (2%)
    pallas_call x1, Pallas kernels, shards(): pl.pallas_call(functools.partial(kernel, INPUTS + FIRST_OUTPUTS + tuple(s...  71.6 us
    pallas_call x1, Pallas kernels, shards(): pl.pallas_call(functools.partial(finish, FINISH_INPUTS + OUTPUTS), out_sh...  2.75 us

profile of v3, /device:TPU:0, one launch (start us, length us, event | category | flops | bytes accessed | tf_op | source)
XLA Modules:
  0.0 75.8 jit_solution(18333342234036125406)
XLA Ops:
  1.3 71.6 %layers.1 = (bf16[64,2048]{1,0:T(8,128)(2,1)}, f32[64,2048]{1,0:T(8,128)}, f32[64,2048]{1,0:T(8,128)}, f32[2,8,32,128]{3,2,1,0:T(8,128)}) custom-call(bf16[64,2048]{1,0:T(8,128)(2,1)} %bitcast.13, bf16[64,2048]{1,0:T(8,128)(2,1)} %bitcast.14, bf16[2,8,64,2048]{3,2,1,0:T(8,128)(2,1)} %bitcast.12, s32[2,8,2048]{2,1,0:T(8,128)} %bitcast.16, s32[4,128]{1,0:T(4,128)} %refs_4_.1, ...), custom_call_target="tpu_custom_call" | custom-call | tf_op jit(solution)/shard_map/layers/pallas_call | solution.py:776
  73.0 2.7 %finish.1 = (bf16[64,2048]{1,0:T(8,128)(2,1)}, f32[64,2048]{1,0:T(8,128)}, f32[64,2048]{1,0:T(8,128)}, f32[2,64,192]{2,1,0:T(8,128)}, f32[2,64]{1,0:T(2,128)}, /...) custom-call(bf16[64,2048]{1,0:T(8,128)(2,1)} %get-tuple-element.30.r, ...), custom_call_target="tpu_custom_call" | custom-call | tf_op jit(solution)/shard_map/finish/pallas_call | solution.py:806
